TPU v7x, 128 devices: a whole 4x4x4 slice. The times are simulated.
128 devices in a mesh: tensor: 8 (over y, core), seq: 16 (over x, z).
Axes of the slice: x: 4, y: 4, z: 4, core: 2. Of those that a mesh axis runs over, the one named last changes fastest.
Arguments:
- tap_low: bfloat16 [8192, 4096], P('seq', 'tensor'), may hold values from -6 to 6
- tap_mid: bfloat16 [8192, 4096], P('seq', 'tensor'), may hold values from -6 to 6
- residual_in: bfloat16 [8192, 4096], P('seq', 'tensor'), may hold values from -3 to 3
- ffn_act: bfloat16 [8192, 14336], P('seq', 'tensor'), may hold values from -127 to 127, as said below
- act_scale: float32 [8192], P('seq'), may hold values from 0.0020044593 to 0.03006689
- down_codes: bfloat16 [14336, 4096], P('tensor'), may hold values from -127 to 127, as said below
- down_scale: int32 [4096], replicated, may hold values from 32 to 319
- join_weight: bfloat16 [12288, 4096], P('seq', 'tensor'), may hold values from -0.0546875 to 0.0546875
- join_gain: float32 [4096], P('tensor'), may hold values from 0.1 to 1.9
- grad_out: bfloat16 [8192, 4096], P('seq', 'tensor'), may hold values from -0.06591797 to 0.06591797
Outputs:
- drafted: bfloat16 [8192, 4096], P('seq', 'tensor')
- grad_join: bfloat16 [12288, 4096], P('seq', 'tensor')
Inputs may be any that keep to these rules, and one draw needn't show every extreme that they name: `ffn_act`: whole numbers. `down_codes`: whole numbers.
All inputs are finite; a program needn't handle non-finite values.
Results may differ from a plain program's by a relative error of at most 0.019.
Values may be sent and summed in bfloat16 or wider, within the bound.
A program may use at most 128 MiB of HBM per device.

v0:
```python
import jax
import jax.numpy as jnp
from jax import lax
from jax.sharding import PartitionSpec as P

D = 4096


QUANT_UNIT = 2.0 ** (-19)


def on_device(
    tap_low,
    tap_mid,
    residual_in,
    ffn_act,
    act_scale,
    down_codes,
    down_scale,
    join_weight,
    join_gain,
    grad_out,
):
    slice_width = tap_low.shape[1]
    col_full = down_scale.astype(jnp.float32) * QUANT_UNIT
    row_scale = act_scale[:, None]
    local_sum = jnp.dot(ffn_act, down_codes, preferred_element_type=jnp.float32)
    down_part = lax.psum_scatter(local_sum, "tensor", scatter_dimension=1, tiled=True)
    own_scale = lax.dynamic_slice_in_dim(
        col_full, lax.axis_index("tensor") * slice_width, slice_width
    )
    tap_high = (
        residual_in.astype(jnp.float32) + down_part * row_scale * own_scale[None, :]
    ).astype(jnp.bfloat16)
    low_full, mid_full, high_full = (
        lax.all_gather(tap_low, "tensor", axis=1, tiled=True),
        lax.all_gather(tap_mid, "tensor", axis=1, tiled=True),
        lax.all_gather(tap_high, "tensor", axis=1, tiled=True),
    )
    tapped = jnp.concatenate([low_full, mid_full, high_full], axis=1)
    columns = tapped
    joined_sum = jnp.dot(
        columns,
        lax.all_gather(join_weight, "seq", axis=0, tiled=True),
        preferred_element_type=jnp.float32,
    )
    squares = lax.psum(jnp.sum(joined_sum * joined_sum, axis=1), "tensor")
    inverse_rms = lax.rsqrt(squares / D + 1e-05)[:, None]
    normed = joined_sum * inverse_rms
    drafted = (normed * join_gain[None, :]).astype(jnp.bfloat16)
    grad_norm = grad_out.astype(jnp.float32) * join_gain[None, :]
    inner = lax.psum(jnp.sum(grad_norm * normed, axis=1), "tensor")
    projection = (inner / D)[:, None]
    grad_joined = (inverse_rms * (grad_norm - normed * projection)).astype(jnp.bfloat16)
    columns = tapped
    grad_join = lax.psum_scatter(
        lax.dot_general(
            columns, grad_joined, (((0,), (0,)), ((), ())), preferred_element_type=jnp.float32
        ).astype(jnp.bfloat16),
        "seq",
        scatter_dimension=0,
        tiled=True,
    )
    return (drafted, grad_join)


def solution(mesh):
    return jax.shard_map(
        on_device,
        mesh=mesh,
        in_specs=(
            P("seq", "tensor"),
            P("seq", "tensor"),
            P("seq", "tensor"),
            P("seq", "tensor"),
            P("seq"),
            P("tensor", None),
            P(),
            P("seq", "tensor"),
            P("tensor"),
            P("seq", "tensor"),
        ),
        out_specs=(P("seq", "tensor"), P("seq", "tensor")),
        check_vma=False,
    )
```

profile of v0, /device:TPU:0, one launch (start us, length us, event | category | flops | bytes accessed | tf_op | source)
XLA Modules:
  0.0 423.2 jit_solution(11779592943637058606)
XLA Ops:
  7.2 1.4 copy-done
  8.7 12.9 %fusion.4 = f32[512,4096]{1,0:T(8,128)} fusion(bf16[512,1792]{1,0:T(8,128)(2,1)S(1)} %copy-done, bf16[1792,4096]{1,0:T(8,128)(2,1)} %param.15), kind=kOutput, calls=%fused_computation.17 | convolution fusion | flops 7516192768 | bytes 24903680 | tf_op jit(solution)/shard_map/dot_general | solution.py:27
  21.7 0.7 all-gather.5.cloned.1.call-update
  22.4 0.7 all-gather.7.cloned.1.call-update
  23.2 0.8 fusion.3
  23.9 52.8 %reduce-scatter.3.cloned.1.call-done = f32[512,512]{1,0:T(8,128)} async-done(((f32[512,4096]{1,0:T(8,128)}), f32[512,512]{1,0:T(8,128)}) %reduce-scatter.3.cloned.1.call-update) | async-done | bytes 1048592 | tf_op jit(solution)/shard_map/reduce_scatter | solution.py:28
  76.7 2.2 add_convert_fusion
  79.0 0.0 all-gather.11.cloned.1.call-start
  79.0 0.5 all-gather.11.cloned.1.call-update
  79.6 0.2 copy.12
  79.8 30.3 %all-gather.5.cloned.1.call-done = bf16[512,4096]{1,0:T(8,128)(2,1)} async-done(((bf16[512,512]{1,0:T(8,128)(2,1)}), bf16[512,4096]{1,0:T(8,128)(2,1)}) %all-gather.5.cloned.1.call-update) | async-done | bytes 4194320 | tf_op jit(solution)/shard_map/all_gather | solution.py:36
  110.1 4.7 %constant_dynamic-update-slice_fusion.2 = bf16[512,12288]{1,0:T(8,128)(2,1)} fusion(bf16[512,4096]{1,0:T(8,128)(2,1)} %all-gather.5.cloned.1.call-done), kind=kLoop, calls=%fused_computation.12 | loop fusion | bytes 8388608
  114.9 29.1 %all-gather.7.cloned.1.call-done = bf16[512,4096]{1,0:T(8,128)(2,1)} async-done(((bf16[512,512]{1,0:T(8,128)(2,1)}), bf16[512,4096]{1,0:T(8,128)(2,1)}) %all-gather.7.cloned.1.call-update) | async-done | bytes 4194320 | tf_op jit(solution)/shard_map/all_gather | solution.py:37
  143.9 4.7 %constant_dynamic-update-slice_fusion.1 = bf16[512,12288]{1,0:T(8,128)(2,1)} fusion(bf16[512,12288]{1,0:T(8,128)(2,1)} %constant_dynamic-update-slice_fusion.2, bf16[512,4096]{1,0:T(8,128)(2,1)} %all-gather.7.cloned.1.call-done), kind=kLoop, calls=%fused_computation.11 | loop fusion | bytes 8388608
  148.7 29.5 %all-gather.9.cloned.1.call-done = bf16[512,4096]{1,0:T(8,128)(2,1)} async-done(((bf16[512,512]{1,0:T(8,128)(2,1)}), bf16[512,4096]{1,0:T(8,128)(2,1)}) %all-gather.9.cloned.1.call-update) | async-done | bytes 4194320 | tf_op jit(solution)/shard_map/all_gather | solution.py:38
  178.2 4.6 %constant_dynamic-update-slice_fusion = bf16[512,12288]{1,0:T(8,128)(2,1)} fusion(bf16[512,12288]{1,0:T(8,128)(2,1)} %constant_dynamic-update-slice_fusion.1, bf16[512,4096]{1,0:T(8,128)(2,1)} %all-gather.9.cloned.1.call-done), kind=kLoop, calls=%fused_computation.10 | loop fusion | bytes 8388608 | tf_op jit(solution)/shard_map/concatenate | solution.py:40
  182.8 87.5 %all-gather.11.cloned.1.call-done = bf16[12288,512]{1,0:T(8,128)(2,1)} async-done(((bf16[768,512]{1,0:T(8,128)(2,1)}), bf16[12288,512]{1,0:T(8,128)(2,1)}) %all-gather.11.cloned.1.call-update) | async-done | bytes 12582928 | tf_op jit(solution)/shard_map/all_gather | solution.py:44
  270.3 11.7 %multiply_reduce_fusion.1 = (f32[512]{0:T(512)S(1)}, f32[512,512]{0,1:T(8,128)S(1)}) fusion(bf16[512,12288]{1,0:T(8,128)(2,1)} %constant_dynamic-update-slice_fusion, bf16[12288,512]{1,0:T(8,128)(2,1)} %all-gather.11.cloned.1.call-done), kind=kOutput, calls=%fused_computation.5 | convolution fusion | flops 6442974720 | bytes 26216448 | tf_op jit(solution)/shard_map/dot_general | solution.py:42
  282.1 14.6 %psum.14 = f32[512]{0:T(512)S(1)} all-reduce(f32[512]{0:T(512)S(1)} %get-tuple-element.6), channel_id=1, replica_groups=mesh['tensor'=8,'seq'=16] {'tensor'}, use_global_device_ids=true, to_apply=%region_2.0 | all-reduce | flops 512 | bytes 4096 | tf_op jit(solution)/shard_map/psum | solution.py:47
  296.7 0.3 multiply_reduce_fusion
  297.0 12.6 %psum.15 = f32[512]{0:T(512)S(1)} all-reduce(f32[512]{0:T(512)S(1)} %get-tuple-element.4), channel_id=1, replica_groups=mesh['tensor'=8,'seq'=16] {'tensor'}, use_global_device_ids=true, to_apply=%region_4.0 | all-reduce | flops 512 | bytes 4096 | tf_op jit(solution)/shard_map/psum | solution.py:52
  309.6 14.8 %convolution_convert_fusion = bf16[12288,512]{1,0:T(8,128)(2,1)} fusion(bf16[512,12288]{1,0:T(8,128)(2,1)} %constant_dynamic-update-slice_fusion, bf16[512,512]{0,1:T(8,128)(2,1)S(1)} %copy.12, f32[512,512]{0,1:T(8,128)} %copy-done.2, f32[512]{0:T(512)S(1)} %broadcast_multiply_fusion, f32[512]{0:T(512)S(1)} %copy-done.5, f32[512]{0:T(512)S(1)} %add_rsqrt_fusion), kind=kOutput, calls=%fused_computation | convolution fusion | flops 6450577408 | bytes 26744832 | tf_op jit(solution)/shard_map/dot_general | solution.py:57
  324.4 1.0 copy.13
  325.4 90.9 %reduce-scatter.5.cloned.1.call-done = bf16[768,512]{1,0:T(8,128)(2,1)} async-done(((bf16[12288,512]{1,0:T(8,128)(2,1)}), bf16[768,512]{1,0:T(8,128)(2,1)}) %reduce-scatter.5.cloned.1.call-update) | async-done | bytes 786448 | tf_op jit(solution)/shard_map/reduce_scatter | solution.py:56
  (23 shorter events, 0.3 us)
Async XLA Ops:
  7.2 1.5 copy-start
  7.2 69.5 %copy-start.4 = (bf16[512,512]{1,0:T(8,128)(2,1)S(1)}, bf16[512,512]{1,0:T(8,128)(2,1)}, u32[]{:S(2)}) copy-start(bf16[512,512]{1,0:T(8,128)(2,1)} %param.12) | copy-start | bytes 1572868
  7.2 69.5 %copy-start.6 = (f32[512]{0:T(512)S(1)}, f32[512]{0:T(512)}, u32[]{:S(2)}) copy-start(f32[512]{0:T(512)} %param.14) | copy-start | bytes 6148
  7.2 69.5 %reduce-scatter.3.cloned.1.call-start = ((), (), s32[]{:S(2)}) async-start(), calls=%async_computation.4 | async-start | bytes 9437184 | tf_op jit(solution)/shard_map/reduce_scatter | solution.py:28
  21.6 58.0 %copy-start.3 = (bf16[512,512]{1,0:T(8,128)(2,1)S(1)}, bf16[512,512]{1,0:T(8,128)(2,1)}, u32[]{:S(2)}) copy-start(bf16[512,512]{1,0:T(8,128)(2,1)} %param.19) | copy-start | bytes 1572868
  21.6 88.5 %all-gather.5.cloned.1.call-start = ((), (), s32[]{:S(2)}) async-start(), calls=%async_computation.2 | async-start | bytes 4718592 | tf_op jit(solution)/shard_map/all_gather | solution.py:36
  22.4 121.5 %all-gather.7.cloned.1.call-start = ((), (), s32[]{:S(2)}) async-start(), calls=%async_computation.3 | async-start | bytes 4718592 | tf_op jit(solution)/shard_map/all_gather | solution.py:37
  23.1 155.0 %all-gather.9.cloned.1.call-start = ((), (), s32[]{:S(2)}) async-start(), calls=%async_computation.5 | async-start | bytes 4718592 | tf_op jit(solution)/shard_map/all_gather | solution.py:38
  79.0 191.3 %all-gather.11.cloned.1.call-start = ((), (), s32[]{:S(2)}) async-start(), calls=%async_computation.6 | async-start | bytes 13369344 | tf_op jit(solution)/shard_map/all_gather | solution.py:44
  79.6 336.7 %reduce-scatter.5.cloned.1.call-start = ((), (), s32[]{:S(2)}) async-start(), calls=%async_computation.7 | async-start | bytes 13369344 | tf_op jit(solution)/shard_map/reduce_scatter | solution.py:56
  182.8 113.9 %copy-start.5 = (f32[512]{0:T(512)S(1)}, f32[512]{0:T(512)}, u32[]{:S(2)}) copy-start(f32[512]{0:T(512)} %param.18) | copy-start | bytes 6148
  282.1 14.6 %copy-start.2 = (f32[512,512]{0,1:T(8,128)}, f32[512,512]{0,1:T(8,128)S(1)}, u32[]{:S(2)}) copy-start(f32[512,512]{0,1:T(8,128)S(1)} %get-tuple-element.7) | copy-start | bytes 3145732
  309.6 106.7 %copy-start.1 = (bf16[512,1792]{1,0:T(8,128)(2,1)S(1)}, bf16[512,1792]{1,0:T(8,128)(2,1)}, u32[]{:S(2)}) copy-start(bf16[512,1792]{1,0:T(8,128)(2,1)} %param.13) | copy-start | bytes 5505028
Sparse Core Ops, SparseCore 0:
  21.8 54.9 reduce-scatter.2
  78.4 31.6 all-gather.4
  111.8 32.0 all-gather.6
  146.1 32.0 all-gather.8
  180.2 90.0 all-gather.10
  324.6 91.7 reduce-scatter.4
where the time goes:
time: 424 us; the launch traced here: 423 us
  waiting for transfers between devices  322 us (76%)
  matrix products  39.5 us (9%)
  blocking collectives  27.2 us (6%)
  local copies, waits for them, and re-layouts  16.8 us (4%)
  between operations  14.2 us (3%)
    reduce_scatter x1, waiting for transfers between devices, on_device(): lax.psum_scatter(lax.dot_general(columns, grad_joined, (((0,), (0,)), (()...  90.9 us
    all_gather x1, waiting for transfers between devices, on_device(): lax.all_gather(join_weight, 'seq', axis=0, tiled=True)  87.5 us
    reduce_scatter x1, waiting for transfers between devices, on_device(): lax.psum_scatter(local_sum, 'tensor', scatter_dimension=1, tiled=True)  52.8 us
    all_gather x1, waiting for transfers between devices, on_device(): lax.all_gather(tap_low, 'tensor', axis=1, tiled=True)  30.3 us
    all_gather x1, waiting for transfers between devices, on_device(): lax.all_gather(tap_high, 'tensor', axis=1, tiled=True)  29.5 us
    all_gather x1, waiting for transfers between devices, on_device(): lax.all_gather(tap_mid, 'tensor', axis=1, tiled=True)  29.1 us
    dot_general x1, matrix products, on_device(): lax.dot_general(columns, grad_joined, (((0,), (0,)), ((), ())), preferred...  14.8 us
    psum x1, blocking collectives, on_device(): squares = lax.psum(jnp.sum(joined_sum * joined_sum, axis=1), 'tensor')  14.6 us
  transfers between devices with their start and end apart: 6, of which 6 were waited for; matrix products, arithmetic and copies ran while one was open for 4% of the time, Pallas kernels for 0%

commit v1 on v0

v1 whole, which is shorter than its diff:
```python
import functools

import jax
import jax.numpy as jnp
from jax import lax
from jax.experimental import pallas as pl
from jax.experimental.pallas import tpu as pltpu
from jax.sharding import PartitionSpec as P

D = 4096
QUANT_UNIT = 2.0 ** (-19)
BF = jnp.bfloat16
F32 = jnp.float32
TOK = 512
COL = 512
UNIT = 256
HID = 1792
SLOTS = 4
CHUNKS = 2
CW = COL // CHUNKS
XB = 3 * UNIT
MESH = pl.DeviceIdType.MESH


def dot(a, b):
    return jnp.dot(a, b, preferred_element_type=F32)


def body(
    tap_low, tap_mid, residual, act, act_scale, codes, col_code, weight, gain, grad_out,
    drafted, grad_join,
    act_v, codes_v, col_v, res_v, go_v, taps, wts, acc,
    d_own, d_ps, d_pr, d_hs, d_hr, d_bs, d_br, high_v,
    j_hs, j_hr, j_bs, j_br, j_v, st_s, st_r, drafted_v,
    gt_v, g_own, g_hs, g_hr, g_bs, g_br, f_s,
    l_sem, c_sem,
    t_recv, t_zs, t_ys, t_fs, t_ps,
    w_own, w_as, w_side, w_d2, w_ss, w_fs,
    dp_recv, dp_send, dh_recv, dh_send, db_recv, db_send,
    jh_recv, jh_send, jb_recv, jb_send,
    st_recv, st_send,
    ga_side, ga_d2, ga_ss, ga_fs,
    gh_recv, gh_send, gb_recv, gb_send,
    f_recv, f_send,
):
    s = lax.axis_index("seq")
    t = lax.axis_index("tensor")
    x, z = lax.div(s, 4), lax.rem(s, 4)
    y, c = lax.div(t, 2), lax.rem(t, 2)

    def wrap(v):
        return lax.rem(v + 4, 4)

    def dev(xx, zz, yy, cc):
        return {"tensor": 2 * yy + cc, "seq": 4 * xx + zz}

    partner = dev(x, z, y, 1 - c)
    y_to = (dev(x, z, wrap(y + 1), c), dev(x, z, wrap(y - 1), c))
    z_to = (dev(x, wrap(z + 1), y, c), dev(x, wrap(z - 1), y, c))
    x_to = (dev(wrap(x + 1), z, y, c), dev(wrap(x - 1), z, y, c))

    sent = []

    def remote(src, dst, send_sem, recv_sem, device):
        return pltpu.make_async_remote_copy(
            src_ref=src, dst_ref=dst, send_sem=send_sem, recv_sem=recv_sem,
            device_id=device, device_id_type=MESH,
        )

    def send(src, dst, send_sem, recv_sem, device):
        copy = remote(src, dst, send_sem, recv_sem, device)
        copy.start()
        sent.append(copy)

    def arrived(dst, sem):
        pltpu.make_async_copy(dst, dst, sem).wait()

    def send_or_copy(src, dst, send_sem, recv_sem, device, own):
        copy = remote(src, dst, send_sem, recv_sem, device)

        @pl.when(own)
        def _():
            pltpu.make_async_copy(src, dst, recv_sem).start()

        @pl.when(jnp.logical_not(own))
        def _():
            copy.start()

        return copy, own

    branched = []

    def code_block(i):
        dy = (2, 1, 3, 0)[i // 2]
        cc = 1 - c if i % 2 == 0 else c
        return 2 * wrap(y + dy) + cc

    def code_copy(i):
        cols = pl.ds(pl.multiple_of(code_block(i) * COL, COL), COL)
        return pltpu.make_async_copy(codes.at[:, cols], codes_v.at[i % SLOTS], c_sem.at[i % SLOTS])

    act_copy = pltpu.make_async_copy(act, act_v, l_sem.at[0])
    act_copy.start()
    for i in range(SLOTS):
        code_copy(i).start()
    res_copy = pltpu.make_async_copy(residual, res_v, l_sem.at[1])
    res_copy.start()
    go_copy = pltpu.make_async_copy(grad_out, go_v, l_sem.at[2])
    go_copy.start()
    col_copy = pltpu.make_async_copy(
        col_code.at[:, pl.ds(pl.multiple_of(t * COL, COL), COL)], col_v, l_sem.at[3]
    )
    col_copy.start()

    barrier = pltpu.get_barrier_semaphore()
    greeted = 0
    for r in range(1, 8):
        pl.semaphore_signal(
            barrier, inc=1, device_id={"tensor": lax.rem(t + r, 8), "seq": s}, device_id_type=MESH
        )
        greeted += 1
    for r in range(1, 4):
        for cc in range(2):
            pl.semaphore_signal(
                barrier, inc=1, device_id=dev(x, wrap(z + r), y, cc), device_id_type=MESH
            )
            greeted += 1
    for device in x_to:
        pl.semaphore_signal(barrier, inc=1, device_id=device, device_id_type=MESH)
        greeted += 1
    pl.semaphore_wait(barrier, greeted)

    def piece(a, ys, zs):
        rows = pl.ds(pl.multiple_of(zs * TOK, TOK), TOK)
        cols = pl.ds(pl.multiple_of((4 * a + ys) * UNIT, UNIT), UNIT)
        return taps.at[rows, cols]

    def tap_out(a, src):
        for e in range(2):
            zd = 2 * c + e
            branched.append(
                send_or_copy(
                    src.at[:, pl.ds(e * UNIT, UNIT)], piece(a, y, z), t_zs.at[a, e],
                    t_recv.at[a, y, z], dev(x, zd, y, lax.div(z, 2)), zd == z,
                )
            )

    def tap_share(a, dy, k):
        ys, zs = wrap(y + dy), 2 * c + k
        here = piece(a, ys, zs)
        send(here, here, t_ps.at[a, dy, k], t_recv.at[a, ys, zs], partner)

    def tap_own(a):
        for k in range(2):
            zs = 2 * c + k
            here = piece(a, y, zs)
            arrived(here, t_recv.at[a, y, zs])
            for way in range(2):
                send(here, here, t_ys.at[a, k, way], t_recv.at[a, y, zs], y_to[way])
        for k in range(2):
            tap_share(a, 0, k)

    def tap_sides(a):
        for way in range(2):
            ys, zs = wrap(y + (3, 1)[way]), 2 * c + way
            here = piece(a, ys, zs)
            arrived(here, t_recv.at[a, ys, zs])
            send(here, here, t_fs.at[a, way], t_recv.at[a, ys, zs], y_to[way])
        for way in range(2):
            dy = (3, 1)[way]
            ys, zs = wrap(y + dy), 2 * c + 1 - way
            arrived(piece(a, ys, zs), t_recv.at[a, ys, zs])
            tap_share(a, dy, way)
            tap_share(a, dy, 1 - way)

    def tap_far(a):
        ys = wrap(y + 2)
        for k in range(2):
            zs = 2 * c + k
            arrived(piece(a, ys, zs), t_recv.at[a, ys, zs])
            tap_share(a, 2, k)

    def tap_partner(a, zs):
        for dy in (0, 1, 3, 2):
            ys = wrap(y + dy)
            arrived(piece(a, ys, zs), t_recv.at[a, ys, zs])

    def w_rows(xx, i, half=None):
        if half is None:
            return wts.at[pl.ds(pl.multiple_of((3 * xx + i) * UNIT, UNIT), UNIT)]
        h = UNIT // 2
        return wts.at[pl.ds(pl.multiple_of((3 * xx + i) * UNIT + half * h, h), h)]

    def w_out():
        for e in range(3):
            q = 3 * z + e
            zd, i = lax.rem(q, 4), lax.div(q, 4)
            branched.append(
                send_or_copy(
                    weight.at[pl.ds(e * UNIT, UNIT)], w_rows(x, i), w_as.at[e], w_own.at[i],
                    dev(x, zd, y, c), zd == z,
                )
            )

    def w_sides():
        for i in range(3):
            arrived(w_rows(x, i), w_own.at[i])
            for way in range(2):
                send(w_rows(x, i), w_rows(x, i), w_ss.at[i, way], w_side.at[i, way], x_to[way])

    def w_forward():
        for i in range(3):
            for way in range(2):
                xx = wrap(x + (3, 1)[way])
                arrived(w_rows(xx, i), w_side.at[i, way])
                half = w_rows(xx, i, way)
                send(half, half, w_fs.at[i, way], w_d2.at[i, way], x_to[way])

    def w_far():
        for i in range(3):
            for way in range(2):
                arrived(w_rows(wrap(x + 2), i, way), w_d2.at[i, way])

    tap_out(0, tap_low)
    tap_out(1, tap_mid)
    w_out()

    def down_block(i):
        code_copy(i).wait()
        part = dot(act_v[...], codes_v[i % SLOTS])
        n = i // 2
        if i % 2 == 0:
            d_ps[n] = part.astype(BF)
            send(d_ps.at[n], d_pr.at[n], dp_send.at[n], dp_recv.at[n], partner)
        else:
            d_own[n] = part
        if i + SLOTS < 8:
            code_copy(i + SLOTS).start()

    H = TOK // 2
    act_copy.wait()
    down_block(0)
    down_block(1)
    tap_own(0)
    down_block(2)
    arrived(d_pr.at[0], dp_recv.at[0])
    for way in range(2):
        rows = slice(way * H, way * H + H)
        d_hs[way] = (d_own[0, rows] + d_pr[0, rows].astype(F32)).astype(BF)
        send(d_hs.at[way], d_hr.at[way], dh_send.at[way], dh_recv.at[way], y_to[way])
    down_block(3)
    w_sides()
    down_block(4)
    down_block(5)
    for way in range(2):
        n = 1 + way
        arrived(d_pr.at[n], dp_recv.at[n])
        rows = slice(way * H, way * H + H)
        other = slice((1 - way) * H, (1 - way) * H + H)
        d_bs[way, other] = (d_own[n, other] + d_pr[n, other].astype(F32)).astype(BF)
        arrived(d_hr.at[way], dh_recv.at[way])
        d_bs[way, rows] = (
            d_own[n, rows] + d_pr[n, rows].astype(F32) + d_hr[way].astype(F32)
        ).astype(BF)
        send(d_bs.at[way], d_br.at[way], db_send.at[way], db_recv.at[way], y_to[way])
    down_block(6)
    down_block(7)
    tap_sides(0)
    tap_own(1)
    w_forward()

    arrived(d_pr.at[3], dp_recv.at[3])
    res_copy.wait()
    col_copy.wait()
    col_full = col_v[...].astype(F32) * QUANT_UNIT
    row_full = jnp.broadcast_to(act_scale[...], (128, TOK)).T[:, :1]
    for way in range(2):
        arrived(d_br.at[way], db_recv.at[way])
    down = d_own[3] + d_pr[3].astype(F32) + d_br[0].astype(F32) + d_br[1].astype(F32)
    high_v[...] = (res_v[...].astype(F32) + down * row_full * col_full).astype(BF)
    tap_out(2, high_v)
    tap_far(0)
    tap_sides(1)

    def join_wait(a, zs, k):
        @pl.when(lax.div(zs, 2) != c)
        def _():
            tap_partner(a, zs)

    def join_part(a, zs):
        rows = pl.ds(pl.multiple_of(zs * TOK, TOK), TOK)
        return dot(taps[rows, a * 1024 : (a + 1) * 1024], wts[a * 1024 : (a + 1) * 1024])

    w_far()

    def join_low(k, _):
        zs = wrap(z + k)
        join_wait(0, zs, k)
        acc[pl.ds(pl.multiple_of(zs * TOK, TOK), TOK)] = join_part(0, zs)
        return 0

    lax.fori_loop(0, 4, join_low, 0)
    tap_own(2)
    tap_far(1)

    def join_mid(k, _):
        zs = wrap(z + k)
        join_wait(1, zs, k)
        acc[pl.ds(pl.multiple_of(zs * TOK, TOK), TOK)] += join_part(1, zs)
        return 0

    lax.fori_loop(0, 4, join_mid, 0)
    tap_sides(2)
    tap_far(2)

    def join_high(k):
        zs = wrap(z + k)
        join_wait(2, zs, k)
        return acc[pl.ds(pl.multiple_of(zs * TOK, TOK), TOK)] + join_part(2, zs)

    part = join_high(2).astype(BF)
    for way in range(2):
        j_hs[way] = part[way * H : way * H + H]
        send(j_hs.at[way], j_hr.at[way], jh_send.at[way], jh_recv.at[way], z_to[way])
    for way in range(2):
        rows = slice(way * H, way * H + H)
        other = slice((1 - way) * H, (1 - way) * H + H)
        j_v[...] = join_high((1, 3)[way])
        j_bs[way, other] = j_v[other].astype(BF)
        arrived(j_hr.at[way], jh_recv.at[way])
        j_bs[way, rows] = (j_v[rows] + j_hr[way].astype(F32)).astype(BF)
        send(j_bs.at[way], j_br.at[way], jb_send.at[way], jb_recv.at[way], z_to[way])
    j_v[...] = join_high(0)
    for way in range(2):
        arrived(j_br.at[way], jb_recv.at[way])
    go_copy.wait()

    R = 128

    def sums(i, _):
        rows = pl.ds(pl.multiple_of(i * R, R), R)
        joined = j_v[rows] + j_br[0, rows].astype(F32) + j_br[1, rows].astype(F32)
        j_v[rows] = joined
        grad_norm = go_v[rows].astype(F32) * gain[...]
        lane = lax.broadcasted_iota(jnp.int32, (R, 128), 1)
        squares = jnp.sum(joined * joined, axis=1, keepdims=True)
        inner = jnp.sum(grad_norm * joined, axis=1, keepdims=True)
        both = jnp.where(lane == 0, squares, jnp.where(lane == 1, inner, 0.0))
        st_s[:, rows] = both.T[:8]
        return 0

    lax.fori_loop(0, TOK // R, sums, 0)
    for r in range(1, 8):
        send(
            st_s, st_r.at[r - 1], st_send.at[r - 1], st_recv.at[r - 1],
            {"tensor": lax.rem(t + r, 8), "seq": s},
        )
    for r in range(1, 8):
        arrived(st_r.at[r - 1], st_recv.at[r - 1])

    own_tokens = pl.multiple_of(z * TOK, TOK)

    def norm(i, _):
        rows = pl.ds(pl.multiple_of(i * R, R), R)
        total = st_s[:, rows]
        for r in range(7):
            total = total + st_r[r, :, rows]
        both = jnp.concatenate([total, jnp.zeros((120, R), F32)], axis=0).T
        inverse_rms = lax.rsqrt(both[:, 0:1] / D + 1e-05)
        projection = inverse_rms * both[:, 1:2] / D
        normed = j_v[rows] * inverse_rms
        drafted_v[rows] = (normed * gain[...]).astype(BF)
        grad_norm = go_v[rows].astype(F32) * gain[...]
        grad_joined = inverse_rms * (grad_norm - normed * projection)
        gt_v[:, pl.ds(pl.multiple_of(own_tokens + i * R, R), R)] = grad_joined.T.astype(BF)
        return 0

    lax.fori_loop(0, TOK // R, norm, 0)

    CH = CW // 2

    def g_piece(n, zs, half=None):
        cols = pl.ds(pl.multiple_of(zs * TOK, TOK), TOK)
        if half is None:
            return gt_v.at[pl.ds(n * CW, CW), cols]
        return gt_v.at[pl.ds(n * CW + half * CH, CH), cols]

    for n in range(CHUNKS):
        for way in range(2):
            send(g_piece(n, z), g_piece(n, z), ga_ss.at[n, way], ga_side.at[n, way], z_to[way])
    drafted_copy = pltpu.make_async_copy(drafted_v, drafted, l_sem.at[4])
    drafted_copy.start()

    def g_forward(n):
        for way in range(2):
            zs = wrap(z + (3, 1)[way])
            arrived(g_piece(n, zs), ga_side.at[n, way])
            send(g_piece(n, zs, way), g_piece(n, zs, way), ga_fs.at[n, way], ga_d2.at[n, way], z_to[way])

    def grad_part(n, dx):
        cols = pl.ds(pl.multiple_of(wrap(x + dx) * XB, XB), XB)
        return dot(gt_v[n * CW : n * CW + CW], taps[:, cols])

    def grad_start(n):
        for way in range(2):
            arrived(g_piece(n, wrap(z + 2), way), ga_d2.at[n, way])
        part = grad_part(n, 2).astype(BF)
        for way in range(2):
            g_hs[n, way] = part[way * CH : way * CH + CH]
            send(g_hs.at[n, way], g_hr.at[n, way], gh_send.at[n, way], gh_recv.at[n, way], x_to[way])

    def grad_sides(n):
        for way in range(2):
            part = grad_part(n, (1, 3)[way])
            arrived(g_hr.at[n, way], gh_recv.at[n, way])
            for half in range(2):
                rows = slice(half * CH, half * CH + CH)
                value = part[rows]
                if half == way:
                    value = value + g_hr[n, way].astype(F32)
                g_bs[n, way, rows] = value.astype(BF)
            send(g_bs.at[n, way], g_br.at[n, way], gb_send.at[n, way], gb_recv.at[n, way], x_to[way])
        g_own[n] = grad_part(n, 0)

    def grad_end(n):
        for way in range(2):
            arrived(g_br.at[n, way], gb_recv.at[n, way])
        for i in range(3):
            rows = slice(i * UNIT, i * UNIT + UNIT)
            total = g_own[n, :, rows] + g_br[n, 0, :, rows].astype(F32) + g_br[n, 1, :, rows].astype(F32)
            f_s[n, rows] = total.T.astype(BF)
            q = 4 * i + z
            zd, e = lax.div(q, 3), lax.rem(q, 3)
            dst = grad_join.at[pl.ds(pl.multiple_of(e * UNIT, UNIT), UNIT), pl.ds(n * CW, CW)]
            branched.append(
                send_or_copy(
                    f_s.at[n, pl.ds(i * UNIT, UNIT)], dst, f_send.at[n, i], f_recv.at[n, e],
                    dev(x, zd, y, c), zd == z,
                )
            )

    for n in range(CHUNKS):
        g_forward(n)
    for n in range(CHUNKS):
        grad_start(n)
        grad_sides(n)
    for n in range(CHUNKS):
        grad_end(n)

    for n in range(CHUNKS):
        for e in range(3):
            arrived(grad_join.at[pl.ds(e * UNIT, UNIT), pl.ds(n * CW, CW)], f_recv.at[n, e])
    drafted_copy.wait()
    for copy in sent:
        copy.wait_send()
    for copy, own in branched:

        @pl.when(jnp.logical_not(own))
        def _(copy=copy):
            copy.wait_send()


def on_device(
    tap_low, tap_mid, residual_in, ffn_act, act_scale, down_codes, down_scale,
    join_weight, join_gain, grad_out,
):
    any_ = pl.BlockSpec(memory_space=pl.ANY)
    vmem = pl.BlockSpec(memory_space=pltpu.VMEM)
    V = pltpu.VMEM
    dma = lambda *shape: pltpu.SemaphoreType.DMA(shape)
    half = TOK // 2
    scratch = [
        V((TOK, HID), BF), V((SLOTS, HID, COL), BF), V((1, COL), jnp.int32),
        V((TOK, COL), BF), V((TOK, COL), BF),
        V((4 * TOK, 12 * UNIT), BF), V((12 * UNIT, COL), BF), V((4 * TOK, COL), F32),
        V((4, TOK, COL), F32), V((4, TOK, COL), BF), V((4, TOK, COL), BF),
        V((2, half, COL), BF), V((2, half, COL), BF), V((2, TOK, COL), BF), V((2, TOK, COL), BF),
        V((TOK, COL), BF),
        V((2, half, COL), BF), V((2, half, COL), BF), V((2, TOK, COL), BF), V((2, TOK, COL), BF),
        V((TOK, COL), F32), V((8, TOK), F32), V((7, 8, TOK), F32), V((TOK, COL), BF),
        V((COL, 4 * TOK), BF), V((CHUNKS, CW, XB), F32),
        V((CHUNKS, 2, CW // 2, XB), BF), V((CHUNKS, 2, CW // 2, XB), BF),
        V((CHUNKS, 2, CW, XB), BF), V((CHUNKS, 2, CW, XB), BF),
        V((CHUNKS, XB, CW), BF),
        dma(5), dma(SLOTS),
        dma(3, 4, 4), dma(3, 2), dma(3, 2, 2), dma(3, 2), dma(3, 4, 2),
        dma(3), dma(3), dma(3, 2), dma(3, 2), dma(3, 2), dma(3, 2),
        dma(4), dma(4), dma(2), dma(2), dma(2), dma(2),
        dma(2), dma(2), dma(2), dma(2),
        dma(7), dma(7),
        dma(CHUNKS, 2), dma(CHUNKS, 2), dma(CHUNKS, 2), dma(CHUNKS, 2),
        dma(CHUNKS, 2), dma(CHUNKS, 2), dma(CHUNKS, 2), dma(CHUNKS, 2),
        dma(CHUNKS, 3), dma(CHUNKS, 3),
    ]
    return pl.pallas_call(
        body,
        out_shape=(
            jax.ShapeDtypeStruct((TOK, COL), BF),
            jax.ShapeDtypeStruct((XB, COL), BF),
        ),
        in_specs=[any_, any_, any_, any_, vmem, any_, any_, any_, vmem, any_],
        out_specs=(any_, any_),
        scratch_shapes=scratch,
        compiler_params=pltpu.CompilerParams(
            collective_id=0, has_side_effects=True, vmem_limit_bytes=63 * 1024 * 1024
        ),
        cost_estimate=pl.CostEstimate(
            flops=20_400_000_000, bytes_accessed=30_000_000, transcendentals=0
        ),
        name="tapped_join",
    )(
        tap_low, tap_mid, residual_in, ffn_act, act_scale.reshape(1, TOK), down_codes,
        down_scale.reshape(1, D), join_weight, join_gain.reshape(1, COL), grad_out,
    )


def solution(mesh):
    return jax.shard_map(
        on_device,
        mesh=mesh,
        in_specs=(
            P("seq", "tensor"),
            P("seq", "tensor"),
            P("seq", "tensor"),
            P("seq", "tensor"),
            P("seq"),
            P("tensor", None),
            P(),
            P("seq", "tensor"),
            P("tensor"),
            P("seq", "tensor"),
        ),
        out_specs=(P("seq", "tensor"), P("seq", "tensor")),
        check_vma=False,
    )
```

time: 424 us -> 176 us (0.42)
  waiting for transfers between devices: 322 us -> 0 us
  Pallas kernels: 0 us -> 171 us
  matrix products: 39.5 us -> 0 us
  blocking collectives: 27.2 us -> 0 us
  between operations: 14.2 us -> 0.64 us
  local copies, waits for them, and re-layouts: 16.8 us -> 3.93 us
    all_gather x4 -> x0, waiting for transfers between devices: 176 us -> none  [the longest x1 87.5 us: on_device(): lax.all_gather(join_weight, 'seq', axis=0, tiled=True)]
    pallas_call x0 -> x1, Pallas kernels: none -> 171 us  [on_device(): pl.pallas_call(body, out_shape=(jax.ShapeDtypeStruct((TOK, COL), BF), jax...]
    reduce_scatter x2 -> x0, waiting for transfers between devices: 144 us -> none  [the longest x1 90.9 us: on_device(): lax.psum_scatter(lax.dot_general(columns, grad_joined, (((0,), (0,)), (()...]
    dot_general x3 -> x0, matrix products: 39.5 us -> none  [the longest x1 14.8 us: on_device(): lax.dot_general(columns, grad_joined, (((0,), (0,)), ((), ())), preferred...]
    psum x2 -> x0, blocking collectives: 27.2 us -> none  [the longest x1 14.6 us: on_device(): squares = lax.psum(jnp.sum(joined_sum * joined_sum, axis=1), 'tensor')]
    unnamed x18 -> x2, local copies, waits for them, and re-layouts: 12.1 us -> 3.93 us
    concatenate x1 -> x0, local copies, waits for them, and re-layouts: 4.64 us -> none  [on_device(): tapped = jnp.concatenate([low_full, mid_full, high_full], axis=1)]
  transfers between devices with their start and end apart: 6 -> 0, of which waited for: 6 -> 0; matrix products, arithmetic and copies ran while one was open for 4% -> 0% of each run, Pallas kernels for 0% -> 0%
where the time goes in v1:
time: 176 us
  Pallas kernels  171 us (97%)
  local copies, waits for them, and re-layouts  3.93 us (2%)
    pallas_call x1, Pallas kernels, on_device(): pl.pallas_call(body, out_shape=(jax.ShapeDtypeStruct((TOK, COL), BF), jax...  171 us
    unnamed x2, local copies, waits for them, and re-layouts  3.93 us

profile of v1, /device:TPU:0, one launch (start us, length us, event | category | flops | bytes accessed | tf_op | source)
XLA Modules:
  0.0 175.7 jit_solution(9212065050047246687)
XLA Ops:
  0.6 171.1 %tapped_join.1 = (bf16[512,512]{1,0:T(8,128)(2,1)}, bf16[768,512]{1,0:T(8,128)(2,1)}) custom-call(bf16[512,512]{1,0:T(8,128)(2,1)} %tap_low.1, bf16[512,512]{1,0:T(8,128)(2,1)} %tap_mid.1, bf16[512,512]{1,0:T(8,128)(2,1)} %residual.1, bf16[512,1792]{1,0:T(8,128)(2,1)} %act.1, f32[1,512]{1,0:T(1,128)} %bitcast.4, bf16[1792,4096]{1,0:T(8,128)(2,1)} %codes.1, ...), custom_call_target="tpu_custom_call" | custom-call | flops 20400001024 | bytes 30000000 | tf_op jit(solution)/shard_map/tapped_join/pallas_call | solution.py:495
  171.7 1.9 %copy.14 = bf16[512,512]{1,0:T(8,128)(2,1)} copy(bf16[512,512]{1,0:T(8,128)(2,1)} %get-tuple-element.4) | data formatting | bytes 1048576
  173.6 2.1 %copy.15 = bf16[768,512]{1,0:T(8,128)(2,1)} copy(bf16[768,512]{1,0:T(8,128)(2,1)} %get-tuple-element.5) | data formatting | bytes 1572864

commit v2 on v0

v2 whole, which is shorter than its diff:
```python
import jax
import jax.numpy as jnp
from jax import lax
from jax.experimental import pallas as pl
from jax.experimental.pallas import tpu as pltpu
from jax.sharding import PartitionSpec as P

D = 4096
QUANT_UNIT = 2.0 ** (-19)
BF = jnp.bfloat16
F32 = jnp.float32
TOK = 512
HT = TOK // 2
QT = HT // 2
COL = 512
UNIT = 128
HID = 1792
SLOTS = 4
CHUNKS = 2
CW = COL // CHUNKS
CH = CW // 2
XB = 3 * UNIT
KG = 12 * UNIT
MESH = pl.DeviceIdType.MESH


def dot(a, b):
    return jnp.dot(a, b, preferred_element_type=F32)


def body(
    tap_low, tap_mid, residual, act, act_scale, codes, col_code, weight, gain, grad_out,
    drafted, grad_join,
    act_v, codes_v, col_v, res_v, go_v, taps, wts,
    d_own, d_ps, d_pr, d_hs, d_hr, d_bs, d_br, high_v,
    j_hs, j_hr, j_bs, j_br, j_v, st_s, st_r, drafted_v,
    gt_v, g_own, g_hs, g_hr, g_bs, g_br, f_s,
    l_sem, c_sem,
    t_in, t_side, t_far, t_pp, t_zs, t_ys, t_fs, t_ps,
    w_own, w_as, w_side, w_d2, w_ss, w_fs,
    dp_recv, dp_send, dh_recv, dh_send, db_recv, db_send,
    jh_recv, jh_send, jb_recv, jb_send,
    st_recv, st_send,
    ga_side, ga_d2, ga_ss, ga_fs,
    gh_recv, gh_send, gb_recv, gb_send,
    f_recv, f_send,
):
    s = lax.axis_index("seq")
    t = lax.axis_index("tensor")
    x, z = lax.div(s, 4), lax.rem(s, 4)
    y, c = lax.div(t, 2), lax.rem(t, 2)

    def wrap(v):
        return lax.rem(v + 4, 4)

    def dev(xx, zz, yy, cc):
        return {"tensor": 2 * yy + cc, "seq": 4 * xx + zz}

    partner = dev(x, z, y, 1 - c)
    y_to = (dev(x, z, wrap(y + 1), c), dev(x, z, wrap(y - 1), c))
    z_to = (dev(x, wrap(z + 1), y, c), dev(x, wrap(z - 1), y, c))
    x_to = (dev(wrap(x + 1), z, y, c), dev(wrap(x - 1), z, y, c))
    ring, ring_to = (z, x), (z_to, x_to)
    cross, cross_to = (x, z), (x_to, z_to)

    def on_ring(g, r, cc):
        return dev(x, r, y, cc) if g == 0 else dev(r, z, y, cc)

    sent = []
    branched = []

    def remote(src, dst, send_sem, recv_sem, device):
        return pltpu.make_async_remote_copy(
            src_ref=src, dst_ref=dst, send_sem=send_sem, recv_sem=recv_sem,
            device_id=device, device_id_type=MESH,
        )

    def send(src, dst, send_sem, recv_sem, device):
        copy = remote(src, dst, send_sem, recv_sem, device)
        copy.start()
        sent.append(copy)

    def arrived(dst, sem):
        pltpu.make_async_copy(dst, dst, sem).wait()

    def send_or_copy(src, dst, send_sem, recv_sem, device, own):
        copy = remote(src, dst, send_sem, recv_sem, device)

        @pl.when(own)
        def _():
            pltpu.make_async_copy(src, dst, recv_sem).start()

        @pl.when(jnp.logical_not(own))
        def _():
            copy.start()

        branched.append((copy, own))

    def drain():
        while sent:
            sent.pop(0).wait_send()
        while branched:
            copy, own = branched.pop(0)

            @pl.when(jnp.logical_not(own))
            def _(copy=copy):
                copy.wait_send()

    def code_block(i):
        dy = (2, 1, 3, 0)[i // 2]
        cc = 1 - c if i % 2 == 0 else c
        return 2 * wrap(y + dy) + cc

    def code_copy(i):
        cols = pl.ds(pl.multiple_of(code_block(i) * COL, COL), COL)
        return pltpu.make_async_copy(codes.at[:, cols], codes_v.at[i % SLOTS], c_sem.at[i % SLOTS])

    act_copy = pltpu.make_async_copy(act, act_v, l_sem.at[0])
    act_copy.start()
    for i in range(SLOTS):
        code_copy(i).start()
    res_copy = pltpu.make_async_copy(residual, res_v, l_sem.at[1])
    res_copy.start()
    go_copy = pltpu.make_async_copy(grad_out, go_v, l_sem.at[2])
    go_copy.start()
    col_copy = pltpu.make_async_copy(
        col_code.at[:, pl.ds(pl.multiple_of(t * COL, COL), COL)], col_v, l_sem.at[3]
    )
    col_copy.start()

    barrier = pltpu.get_barrier_semaphore()
    greeted = 0

    def greet(device):
        pl.semaphore_signal(barrier, inc=1, device_id=device, device_id_type=MESH)

    for r in range(1, 8):
        greet({"tensor": lax.rem(t + r, 8), "seq": s})
        greeted += 1
    for g in range(2):
        for r in range(1, 4):
            for cc in range(2):
                greet(on_ring(g, wrap(ring[g] + r), cc))
                greeted += 1
    pl.semaphore_wait(barrier, greeted)

    def place(g, a, ys):
        n = 4 * a + ys
        if g == 0:
            return n
        xo = lax.div(n, 3)
        return 4 * lax.rem(n, 3) + wrap(x - xo)

    def slab(g, a, ys, h, first, count):
        rows = pl.ds(pl.multiple_of((4 * h + first) * HT, HT), count * HT)
        cols = pl.ds(pl.multiple_of(place(g, a, ys) * UNIT, UNIT), UNIT)
        return taps.at[g, rows, cols]

    def tap_out(a, h, src):
        n = 4 * a + y
        for g in range(2):
            for e in range(2):
                j = 2 * c + e
                if g == 0:
                    to, pos = j, n
                else:
                    to, pos = lax.rem(j + lax.div(n, 3), 4), 4 * lax.rem(n, 3) + j
                rows = pl.ds(pl.multiple_of((4 * h + ring[g]) * HT, HT), HT)
                cols = pl.ds(pl.multiple_of(pos * UNIT, UNIT), UNIT)
                send_or_copy(
                    src.at[pl.ds(h * HT, HT), pl.ds((2 * e + g) * UNIT, UNIT)],
                    taps.at[g, rows, cols],
                    t_zs.at[g, a, h, e],
                    t_in.at[g, a, h],
                    on_ring(g, to, lax.div(ring[g], 2)),
                    jnp.logical_and(to == ring[g], lax.div(ring[g], 2) == c),
                )

    def tap_share(g, a, h, dy):
        here = slab(g, a, wrap(y + dy), h, 2 * c, 2)
        send(here, here, t_ps.at[g, a, h, dy], t_pp.at[g, h], partner)

    def tap_own(a, h):
        for g in range(2):
            here = slab(g, a, y, h, 2 * c, 2)
            arrived(here, t_in.at[g, a, h])
            for way in range(2):
                send(here, here, t_ys.at[g, a, h, way], t_side.at[g, a, h, way], y_to[way])
            tap_share(g, a, h, 0)

    def tap_sides(a, h):
        for g in range(2):
            for way in range(2):
                dy = (3, 1)[way]
                ys = wrap(y + dy)
                arrived(slab(g, a, ys, h, 2 * c, 2), t_side.at[g, a, h, way])
                part = slab(g, a, ys, h, 2 * c + way, 1)
                send(part, part, t_fs.at[g, a, h, way], t_far.at[g, a, h], y_to[way])
                tap_share(g, a, h, dy)

    def tap_far(a, h):
        for g in range(2):
            arrived(slab(g, a, wrap(y + 2), h, 2 * c, 2), t_far.at[g, a, h])
            tap_share(g, a, h, 2)

    def tap_partner(h):
        for g in range(2):
            rows = pl.ds(pl.multiple_of((4 * h + 2 * (1 - c)) * HT, HT), 2 * HT)
            arrived(taps.at[g, rows], t_pp.at[g, h])

    def w_rows(g, p, i, half=None):
        if half is None:
            return wts.at[g, pl.ds(pl.multiple_of((3 * p + i) * UNIT, UNIT), UNIT)]
        n = UNIT // 2
        return wts.at[g, pl.ds(pl.multiple_of((3 * p + i) * UNIT + half * n, n), n)]

    def w_out():
        for e in range(3):
            for g in range(2):
                q = 3 * z + e
                if g == 0:
                    to, i = lax.rem(q, 4), lax.div(q, 4)
                else:
                    to, i = lax.rem(q + x, 4), e
                send_or_copy(
                    weight.at[pl.ds((2 * e + g) * UNIT, UNIT)], w_rows(g, cross[g], i),
                    w_as.at[g, e], w_own.at[g, i], on_ring(g, to, c), to == ring[g],
                )

    def w_sides():
        for g in range(2):
            for i in range(3):
                here = w_rows(g, cross[g], i)
                arrived(here, w_own.at[g, i])
                for way in range(2):
                    send(here, here, w_ss.at[g, i, way], w_side.at[g, i, way], cross_to[g][way])

    def w_forward():
        for g in range(2):
            for i in range(3):
                for way in range(2):
                    p = wrap(cross[g] + (3, 1)[way])
                    arrived(w_rows(g, p, i), w_side.at[g, i, way])
                    half = w_rows(g, p, i, way)
                    send(half, half, w_fs.at[g, i, way], w_d2.at[g, i], cross_to[g][way])

    def w_far():
        for g in range(2):
            for i in range(3):
                arrived(w_rows(g, wrap(cross[g] + 2), i), w_d2.at[g, i])

    tap_out(0, 0, tap_low)
    tap_out(1, 0, tap_mid)
    w_out()
    tap_out(0, 1, tap_low)
    tap_out(1, 1, tap_mid)

    def down_block(i):
        code_copy(i).wait()
        part = dot(act_v[...], codes_v[i % SLOTS])
        n = i // 2
        if i % 2 == 0:
            d_ps[n] = part.astype(BF)
            send(d_ps.at[n], d_pr.at[n], dp_send.at[n], dp_recv.at[n], partner)
        else:
            d_own[n] = part
        if i + SLOTS < 8:
            code_copy(i + SLOTS).start()

    def down_far(h):
        for way in range(2):
            rows = slice(h * HT + way * QT, h * HT + way * QT + QT)
            d_hs[h, way] = (d_own[0, rows] + d_pr[0, rows].astype(F32)).astype(BF)
            send(d_hs.at[h, way], d_hr.at[h, way], dh_send.at[h, way], dh_recv.at[h, way], y_to[way])

    def down_sides(h):
        for way in range(2):
            n = 1 + way
            arrived(d_hr.at[h, way], dh_recv.at[h, way])
            for half in range(2):
                rows = slice(h * HT + half * QT, h * HT + half * QT + QT)
                value = d_own[n, rows] + d_pr[n, rows].astype(F32)
                if half == way:
                    value = value + d_hr[h, way].astype(F32)
                d_bs[h, way, half * QT : half * QT + QT] = value.astype(BF)
            send(d_bs.at[h, way], d_br.at[h, way], db_send.at[h, way], db_recv.at[h, way], y_to[way])

    def down_end(h):
        for way in range(2):
            arrived(d_br.at[h, way], db_recv.at[h, way])
        rows = slice(h * HT, h * HT + HT)
        row_full = jnp.broadcast_to(act_scale[:, rows], (128, HT)).T[:, :1]
        col_full = col_v[...].astype(F32) * QUANT_UNIT
        down = d_own[3, rows] + d_pr[3, rows].astype(F32)
        down = down + d_br[h, 0].astype(F32) + d_br[h, 1].astype(F32)
        high_v[rows] = (res_v[rows].astype(F32) + down * row_full * col_full).astype(BF)
        tap_out(2, h, high_v)

    def joined_part(g, h, r):
        rows = pl.ds(pl.multiple_of((4 * h + wrap(ring[g] + r)) * HT, HT), HT)
        return dot(taps[g, rows], wts[g])

    def join_start(h):
        for g in range(2):
            part = joined_part(g, h, 2).astype(BF)
            for way in range(2):
                j_hs[g, h, way] = part[way * QT : way * QT + QT]
                send(
                    j_hs.at[g, h, way], j_hr.at[g, h, way], jh_send.at[g, h, way],
                    jh_recv.at[g, h, way], ring_to[g][way],
                )

    def join_sides(h):
        for g in range(2):
            for way in range(2):
                part = joined_part(g, h, (1, 3)[way])
                arrived(j_hr.at[g, h, way], jh_recv.at[g, h, way])
                for half in range(2):
                    rows = slice(half * QT, half * QT + QT)
                    value = part[rows]
                    if half == way:
                        value = value + j_hr[g, h, way].astype(F32)
                    j_bs[g, h, way, rows] = value.astype(BF)
                send(
                    j_bs.at[g, h, way], j_br.at[g, h, way], jb_send.at[g, h, way],
                    jb_recv.at[g, h, way], ring_to[g][way],
                )

    def join_own(h):
        j_v[h * HT : h * HT + HT] = joined_part(0, h, 0) + joined_part(1, h, 0)

    def join_end(h):
        for g in range(2):
            for way in range(2):
                arrived(j_br.at[g, h, way], jb_recv.at[g, h, way])
        for i in range(2):
            own = slice(i * QT, i * QT + QT)
            rows = slice(h * HT + i * QT, h * HT + i * QT + QT)
            joined = j_v[rows]
            for g in range(2):
                for way in range(2):
                    joined = joined + j_br[g, h, way, own].astype(F32)
            j_v[rows] = joined
            grad_norm = go_v[rows].astype(F32) * gain[...]
            lane = lax.broadcasted_iota(jnp.int32, (QT, 128), 1)
            squares = jnp.sum(joined * joined, axis=1, keepdims=True)
            inner = jnp.sum(grad_norm * joined, axis=1, keepdims=True)
            both = jnp.where(lane == 0, squares, jnp.where(lane == 1, inner, 0.0))
            st_s[h, :, own] = both.T[:8]
        for r in range(1, 8):
            send(
                st_s.at[h], st_r.at[h, r - 1], st_send.at[h, r - 1], st_recv.at[h, r - 1],
                {"tensor": lax.rem(t + r, 8), "seq": s},
            )

    def g_piece(g, h, n, r, half=None):
        cols = pl.ds(pl.multiple_of((4 * h + r) * HT, HT), HT)
        if half is None:
            return gt_v.at[g, pl.ds(n * CW, CW), cols]
        return gt_v.at[g, pl.ds(n * CW + half * CH, CH), cols]

    def norm(h):
        for r in range(1, 8):
            arrived(st_r.at[h, r - 1], st_recv.at[h, r - 1])
        for i in range(2):
            own = slice(i * QT, i * QT + QT)
            rows = slice(h * HT + i * QT, h * HT + i * QT + QT)
            total = st_s[h, :, own]
            for r in range(7):
                total = total + st_r[h, r, :, own]
            both = jnp.concatenate([total, jnp.zeros((120, QT), F32)], axis=0).T
            inverse_rms = lax.rsqrt(both[:, 0:1] / D + 1e-05)
            projection = inverse_rms * both[:, 1:2] / D
            normed = j_v[rows] * inverse_rms
            drafted_v[rows] = (normed * gain[...]).astype(BF)
            grad_norm = go_v[rows].astype(F32) * gain[...]
            grad_joined = inverse_rms * (grad_norm - normed * projection)
            turned = grad_joined.T.astype(BF)
            for g in range(2):
                gt_v[g, :, pl.ds(pl.multiple_of((4 * h + ring[g]) * HT + i * QT, QT), QT)] = turned
        for n in range(CHUNKS):
            for g in range(2):
                here = g_piece(g, h, n, ring[g])
                for way in range(2):
                    send(here, here, ga_ss.at[g, h, n, way], ga_side.at[g, h, n, way], ring_to[g][way])

    def g_forward(h, n):
        for g in range(2):
            for way in range(2):
                r = wrap(ring[g] + (3, 1)[way])
                arrived(g_piece(g, h, n, r), ga_side.at[g, h, n, way])
                part = g_piece(g, h, n, r, way)
                send(part, part, ga_fs.at[g, h, n, way], ga_d2.at[g, h, n], ring_to[g][way])

    def grad_part(g, n, p):
        cols = pl.ds(pl.multiple_of(wrap(cross[g] + p) * XB, XB), XB)
        return dot(gt_v[g, n * CW : n * CW + CW], taps[g, :, cols])

    def grad_start(n):
        for g in range(2):
            for h in range(2):
                arrived(g_piece(g, h, n, wrap(ring[g] + 2)), ga_d2.at[g, h, n])
            part = grad_part(g, n, 2).astype(BF)
            for way in range(2):
                g_hs[g, n, way] = part[way * CH : way * CH + CH]
                send(
                    g_hs.at[g, n, way], g_hr.at[g, n, way], gh_send.at[g, n, way],
                    gh_recv.at[g, n, way], cross_to[g][way],
                )

    def grad_sides(n):
        for g in range(2):
            for way in range(2):
                part = grad_part(g, n, (1, 3)[way])
                arrived(g_hr.at[g, n, way], gh_recv.at[g, n, way])
                for half in range(2):
                    rows = slice(half * CH, half * CH + CH)
                    value = part[rows]
                    if half == way:
                        value = value + g_hr[g, n, way].astype(F32)
                    g_bs[g, n, way, rows] = value.astype(BF)
                send(
                    g_bs.at[g, n, way], g_br.at[g, n, way], gb_send.at[g, n, way],
                    gb_recv.at[g, n, way], cross_to[g][way],
                )

    def grad_own(n):
        for g in range(2):
            g_own[g, n] = grad_part(g, n, 0)

    def grad_end(n):
        for g in range(2):
            for way in range(2):
                arrived(g_br.at[g, n, way], gb_recv.at[g, n, way])
            total = g_own[g, n] + g_br[g, n, 0].astype(F32) + g_br[g, n, 1].astype(F32)
            f_s[g, n] = total.T.astype(BF)
            for i in range(3):
                if g == 0:
                    q = 4 * i + z
                    to, e = lax.div(q, 3), lax.rem(q, 3)
                else:
                    to, e = wrap(x + z - i), i
                rows = pl.ds(pl.multiple_of((2 * e + g) * UNIT, UNIT), UNIT)
                send_or_copy(
                    f_s.at[g, n, pl.ds(i * UNIT, UNIT)],
                    grad_join.at[rows, pl.ds(n * CW, CW)],
                    f_send.at[g, n, i], f_recv.at[g, n, e], on_ring(g, to, c), to == ring[g],
                )

    act_copy.wait()
    down_block(0)
    down_block(1)
    tap_own(0, 0)
    down_block(2)
    arrived(d_pr.at[0], dp_recv.at[0])
    down_far(0)
    down_far(1)
    tap_own(1, 0)
    down_block(3)
    w_sides()
    down_block(4)
    down_block(5)
    for n in (1, 2):
        arrived(d_pr.at[n], dp_recv.at[n])
    down_sides(0)
    down_sides(1)
    down_block(6)
    down_block(7)
    tap_own(0, 1)
    tap_sides(0, 0)
    tap_sides(1, 0)
    w_forward()
    arrived(d_pr.at[3], dp_recv.at[3])
    res_copy.wait()
    col_copy.wait()
    down_end(0)
    tap_own(1, 1)
    down_end(1)
    tap_far(0, 0)
    tap_far(1, 0)
    tap_own(2, 0)
    w_far()
    tap_sides(0, 1)
    tap_own(2, 1)
    tap_sides(1, 1)
    tap_sides(2, 0)
    tap_far(2, 0)
    tap_partner(0)
    go_copy.wait()
    join_start(0)
    join_sides(0)
    join_own(0)
    tap_far(0, 1)
    tap_far(1, 1)
    join_end(0)
    tap_sides(2, 1)
    norm(0)
    tap_far(2, 1)
    tap_partner(1)
    join_start(1)
    join_sides(1)
    join_own(1)
    for n in range(CHUNKS):
        g_forward(0, n)
    join_end(1)
    norm(1)
    drafted_copy = pltpu.make_async_copy(drafted_v, drafted, l_sem.at[4])
    drafted_copy.start()
    for n in range(CHUNKS):
        g_forward(1, n)
    for n in range(CHUNKS):
        grad_start(n)
        grad_sides(n)
        grad_own(n)
    for n in range(CHUNKS):
        grad_end(n)

    drain()
    drafted_copy.wait()
    for n in range(CHUNKS):
        for g in range(2):
            for e in range(3):
                rows = pl.ds((2 * e + g) * UNIT, UNIT)
                arrived(grad_join.at[rows, pl.ds(n * CW, CW)], f_recv.at[g, n, e])


def on_device(
    tap_low, tap_mid, residual_in, ffn_act, act_scale, down_codes, down_scale,
    join_weight, join_gain, grad_out,
):
    any_ = pl.BlockSpec(memory_space=pl.ANY)
    vmem = pl.BlockSpec(memory_space=pltpu.VMEM)
    V = pltpu.VMEM
    dma = lambda *shape: pltpu.SemaphoreType.DMA(shape)
    scratch = [
        V((TOK, HID), BF), V((SLOTS, HID, COL), BF), V((1, COL), jnp.int32),
        V((TOK, COL), BF), V((TOK, COL), BF),
        V((2, 4 * TOK, KG), BF), V((2, KG, COL), BF),
        V((4, TOK, COL), F32), V((4, TOK, COL), BF), V((4, TOK, COL), BF),
        V((2, 2, QT, COL), BF), V((2, 2, QT, COL), BF),
        V((2, 2, HT, COL), BF), V((2, 2, HT, COL), BF),
        V((TOK, COL), BF),
        V((2, 2, 2, QT, COL), BF), V((2, 2, 2, QT, COL), BF),
        V((2, 2, 2, HT, COL), BF), V((2, 2, 2, HT, COL), BF),
        V((TOK, COL), F32), V((2, 8, HT), F32), V((2, 7, 8, HT), F32), V((TOK, COL), BF),
        V((2, COL, 4 * TOK), BF), V((2, CHUNKS, CW, XB), F32),
        V((2, CHUNKS, 2, CH, XB), BF), V((2, CHUNKS, 2, CH, XB), BF),
        V((2, CHUNKS, 2, CW, XB), BF), V((2, CHUNKS, 2, CW, XB), BF),
        V((2, CHUNKS, XB, CW), BF),
        dma(5), dma(SLOTS),
        dma(2, 3, 2), dma(2, 3, 2, 2), dma(2, 3, 2), dma(2, 2),
        dma(2, 3, 2, 2), dma(2, 3, 2, 2), dma(2, 3, 2, 2), dma(2, 3, 2, 4),
        dma(2, 3), dma(2, 3), dma(2, 3, 2), dma(2, 3), dma(2, 3, 2), dma(2, 3, 2),
        dma(4), dma(4), dma(2, 2), dma(2, 2), dma(2, 2), dma(2, 2),
        dma(2, 2, 2), dma(2, 2, 2), dma(2, 2, 2), dma(2, 2, 2),
        dma(2, 7), dma(2, 7),
        dma(2, 2, CHUNKS, 2), dma(2, 2, CHUNKS), dma(2, 2, CHUNKS, 2), dma(2, 2, CHUNKS, 2),
        dma(2, CHUNKS, 2), dma(2, CHUNKS, 2), dma(2, CHUNKS, 2), dma(2, CHUNKS, 2),
        dma(2, CHUNKS, 3), dma(2, CHUNKS, 3),
    ]
    return pl.pallas_call(
        body,
        out_shape=(
            jax.ShapeDtypeStruct((TOK, COL), BF),
            jax.ShapeDtypeStruct((2 * XB, COL), BF),
        ),
        in_specs=[any_, any_, any_, any_, vmem, any_, any_, any_, vmem, any_],
        out_specs=(any_, any_),
        scratch_shapes=scratch,
        compiler_params=pltpu.CompilerParams(
            collective_id=0, has_side_effects=True, vmem_limit_bytes=63 * 1024 * 1024
        ),
        cost_estimate=pl.CostEstimate(
            flops=20_400_000_000, bytes_accessed=30_000_000, transcendentals=0
        ),
        name="tapped_join",
    )(
        tap_low, tap_mid, residual_in, ffn_act, act_scale.reshape(1, TOK), down_codes,
        down_scale.reshape(1, D), join_weight, join_gain.reshape(1, COL), grad_out,
    )


def solution(mesh):
    return jax.shard_map(
        on_device,
        mesh=mesh,
        in_specs=(
            P("seq", "tensor"),
            P("seq", "tensor"),
            P("seq", "tensor"),
            P("seq", "tensor"),
            P("seq"),
            P("tensor", None),
            P(),
            P("seq", "tensor"),
            P("tensor"),
            P("seq", "tensor"),
        ),
        out_specs=(P("seq", "tensor"), P("seq", "tensor")),
        check_vma=False,
    )
```

time: 424 us -> 170 us (0.40)
  waiting for transfers between devices: 322 us -> 0 us
  Pallas kernels: 0 us -> 165 us
  matrix products: 39.5 us -> 0 us
  blocking collectives: 27.2 us -> 0 us
  between operations: 14.2 us -> 0.64 us
  local copies, waits for them, and re-layouts: 16.8 us -> 3.93 us
    all_gather x4 -> x0, waiting for transfers between devices: 176 us -> none  [the longest x1 87.5 us: on_device(): lax.all_gather(join_weight, 'seq', axis=0, tiled=True)]
    pallas_call x0 -> x1, Pallas kernels: none -> 165 us  [on_device(): pl.pallas_call(body, out_shape=(jax.ShapeDtypeStruct((TOK, COL), BF), jax...]
    reduce_scatter x2 -> x0, waiting for transfers between devices: 144 us -> none  [the longest x1 90.9 us: on_device(): lax.psum_scatter(lax.dot_general(columns, grad_joined, (((0,), (0,)), (()...]
    dot_general x3 -> x0, matrix products: 39.5 us -> none  [the longest x1 14.8 us: on_device(): lax.dot_general(columns, grad_joined, (((0,), (0,)), ((), ())), preferred...]
    psum x2 -> x0, blocking collectives: 27.2 us -> none  [the longest x1 14.6 us: on_device(): squares = lax.psum(jnp.sum(joined_sum * joined_sum, axis=1), 'tensor')]
    unnamed x18 -> x2, local copies, waits for them, and re-layouts: 12.1 us -> 3.93 us
    concatenate x1 -> x0, local copies, waits for them, and re-layouts: 4.64 us -> none  [on_device(): tapped = jnp.concatenate([low_full, mid_full, high_full], axis=1)]
  transfers between devices with their start and end apart: 6 -> 0, of which waited for: 6 -> 0; matrix products, arithmetic and copies ran while one was open for 4% -> 0% of each run, Pallas kernels for 0% -> 0%
where the time goes in v2:
time: 170 us; the launch traced here: 169 us
  Pallas kernels  165 us (97%)
  local copies, waits for them, and re-layouts  3.93 us (2%)
    pallas_call x1, Pallas kernels, on_device(): pl.pallas_call(body, out_shape=(jax.ShapeDtypeStruct((TOK, COL), BF), jax...  165 us
    unnamed x2, local copies, waits for them, and re-layouts  3.93 us

profile of v2, /device:TPU:0, one launch (start us, length us, event | category | flops | bytes accessed | tf_op | source)
XLA Modules:
  0.0 169.2 jit_solution(3420439460257416249)
XLA Ops:
  0.6 164.6 %tapped_join.1 = (bf16[512,512]{1,0:T(8,128)(2,1)}, bf16[768,512]{1,0:T(8,128)(2,1)}) custom-call(bf16[512,512]{1,0:T(8,128)(2,1)} %tap_low.1, bf16[512,512]{1,0:T(8,128)(2,1)} %tap_mid.1, bf16[512,512]{1,0:T(8,128)(2,1)} %residual.1, bf16[512,1792]{1,0:T(8,128)(2,1)} %act.1, f32[1,512]{1,0:T(1,128)} %bitcast.4, bf16[1792,4096]{1,0:T(8,128)(2,1)} %codes.1, ...), custom_call_target="tpu_custom_call" | custom-call | flops 20400001024 | bytes 30000000 | tf_op jit(solution)/shard_map/tapped_join/pallas_call | solution.py:561
  165.3 1.9 %copy.14 = bf16[512,512]{1,0:T(8,128)(2,1)} copy(bf16[512,512]{1,0:T(8,128)(2,1)} %get-tuple-element.4) | data formatting | bytes 1048576
  167.2 2.1 %copy.15 = bf16[768,512]{1,0:T(8,128)(2,1)} copy(bf16[768,512]{1,0:T(8,128)(2,1)} %get-tuple-element.5) | data formatting | bytes 1572864

commit v3 on v2

v3 whole, which is shorter than its diff:
```python
import jax
import jax.numpy as jnp
from jax import lax
from jax.experimental import pallas as pl
from jax.experimental.pallas import tpu as pltpu
from jax.sharding import PartitionSpec as P

D = 4096
QUANT_UNIT = 2.0 ** (-19)
BF = jnp.bfloat16
F32 = jnp.float32
TOK = 512
NQ = 4
QT = TOK // NQ
HT = TOK // 2
FT = HT // 2
COL = 512
UNIT = 128
HID = 1792
SLOTS = 4
CHUNKS = 2
CW = COL // CHUNKS
CH = CW // 2
XB = 3 * UNIT
KG = 12 * UNIT
MESH = pl.DeviceIdType.MESH


def dot(a, b):
    return jnp.dot(a, b, preferred_element_type=F32)


def body(
    tap_low, tap_mid, residual, act, act_scale, codes, col_code, weight, gain, grad_out,
    drafted, grad_join,
    act_v, codes_v, col_v, res_v, go_v, taps, wts,
    d_own, d_ps, d_pr, d_hs, d_hr, d_bs, d_br, high_v,
    j_s, j_r, j_v, st_s, st_r, drafted_v,
    gt_v, g_own, g_hs, g_hr, g_bs, g_br, f_s,
    l_sem, c_sem,
    t_in, t_side, t_far, t_pp, t_zs, t_ys, t_fs, t_ps,
    w_own, w_as, w_side, w_d2, w_ss, w_fs,
    dp_recv, dp_send, dh_recv, dh_send, db_recv, db_send,
    j_recv, j_send, st_recv, st_send, a_recv, a_send,
    gh_recv, gh_send, gb_recv, gb_send,
    f_recv, f_send,
):
    s = lax.axis_index("seq")
    t = lax.axis_index("tensor")
    x, z = lax.div(s, 4), lax.rem(s, 4)
    y, c = lax.div(t, 2), lax.rem(t, 2)

    def wrap(v):
        return lax.rem(v + 4, 4)

    def dev(xx, zz, yy, cc):
        return {"tensor": 2 * yy + cc, "seq": 4 * xx + zz}

    partner = dev(x, z, y, 1 - c)
    y_to = (dev(x, z, wrap(y + 1), c), dev(x, z, wrap(y - 1), c))
    z_to = (dev(x, wrap(z + 1), y, c), dev(x, wrap(z - 1), y, c))
    x_to = (dev(wrap(x + 1), z, y, c), dev(wrap(x - 1), z, y, c))
    ring = (z, x)
    cross, cross_to = (x, z), (x_to, z_to)

    def on_ring(g, r, cc):
        return dev(x, r, y, cc) if g == 0 else dev(r, z, y, cc)

    branched = []

    def remote(src, dst, send_sem, recv_sem, device):
        return pltpu.make_async_remote_copy(
            src_ref=src, dst_ref=dst, send_sem=send_sem, recv_sem=recv_sem,
            device_id=device, device_id_type=MESH,
        )

    def send(src, dst, send_sem, recv_sem, device):
        remote(src, dst, send_sem, recv_sem, device).start()

    def arrived(dst, sem):
        pltpu.make_async_copy(dst, dst, sem).wait()

    def left(src, sem):
        arrived(src, sem)

    def send_or_copy(src, dst, send_sem, recv_sem, device, own):
        copy = remote(src, dst, send_sem, recv_sem, device)

        @pl.when(own)
        def _():
            pltpu.make_async_copy(src, dst, recv_sem).start()

        @pl.when(jnp.logical_not(own))
        def _():
            copy.start()

        branched.append((copy, own))

    def drain():
        while branched:
            copy, own = branched.pop(0)

            @pl.when(jnp.logical_not(own))
            def _(copy=copy):
                copy.wait_send()

    def code_block(i):
        dy = (2, 1, 3, 0)[i // 2]
        cc = 1 - c if i % 2 == 0 else c
        return 2 * wrap(y + dy) + cc

    def code_copy(i):
        cols = pl.ds(pl.multiple_of(code_block(i) * COL, COL), COL)
        return pltpu.make_async_copy(codes.at[:, cols], codes_v.at[i % SLOTS], c_sem.at[i % SLOTS])

    act_copy = pltpu.make_async_copy(act, act_v, l_sem.at[0])
    act_copy.start()
    for i in range(SLOTS):
        code_copy(i).start()
    res_copy = pltpu.make_async_copy(residual, res_v, l_sem.at[1])
    res_copy.start()
    go_copy = pltpu.make_async_copy(grad_out, go_v, l_sem.at[2])
    go_copy.start()
    col_copy = pltpu.make_async_copy(
        col_code.at[:, pl.ds(pl.multiple_of(t * COL, COL), COL)], col_v, l_sem.at[3]
    )
    col_copy.start()

    barrier = pltpu.get_barrier_semaphore()
    greeted = 0

    def greet(device):
        pl.semaphore_signal(barrier, inc=1, device_id=device, device_id_type=MESH)

    for r in range(1, 8):
        greet({"tensor": lax.rem(t + r, 8), "seq": s})
        greeted += 1
    for g in range(2):
        for r in range(1, 4):
            for cc in range(2):
                greet(on_ring(g, wrap(ring[g] + r), cc))
                greeted += 1

    def place(g, a, ys):
        n = 4 * a + ys
        if g == 0:
            return n
        xo = lax.div(n, 3)
        return 4 * lax.rem(n, 3) + wrap(x - xo)

    def slab(g, a, ys, q, first, count):
        rows = pl.ds(pl.multiple_of((4 * q + first) * QT, QT), count * QT)
        cols = pl.ds(pl.multiple_of(place(g, a, ys) * UNIT, UNIT), UNIT)
        return taps.at[g, rows, cols]

    def tap_out(a, q, src):
        n = 4 * a + y
        for g in range(2):
            for e in range(2):
                j = 2 * c + e
                if g == 0:
                    to, pos = j, n
                else:
                    to, pos = lax.rem(j + lax.div(n, 3), 4), 4 * lax.rem(n, 3) + j
                rows = pl.ds(pl.multiple_of((4 * q + ring[g]) * QT, QT), QT)
                cols = pl.ds(pl.multiple_of(pos * UNIT, UNIT), UNIT)
                send_or_copy(
                    src.at[pl.ds(q * QT, QT), pl.ds((2 * e + g) * UNIT, UNIT)],
                    taps.at[g, rows, cols],
                    t_zs.at[g, a, q, e],
                    t_in.at[g, a, q],
                    on_ring(g, to, lax.div(ring[g], 2)),
                    jnp.logical_and(to == ring[g], lax.div(ring[g], 2) == c),
                )

    def tap_share(g, a, q, dy):
        here = slab(g, a, wrap(y + dy), q, 2 * c, 2)
        send(here, here, t_ps, t_pp.at[g, q], partner)

    def tap_own(a, q):
        for g in range(2):
            here = slab(g, a, y, q, 2 * c, 2)
            arrived(here, t_in.at[g, a, q])
            for way in range(2):
                send(here, here, t_ys.at[way], t_side.at[g, a, q, way], y_to[way])
            tap_share(g, a, q, 0)

    def tap_sides(a, q):
        for g in range(2):
            for way in range(2):
                dy = (3, 1)[way]
                ys = wrap(y + dy)
                arrived(slab(g, a, ys, q, 2 * c, 2), t_side.at[g, a, q, way])
                part = slab(g, a, ys, q, 2 * c + way, 1)
                send(part, part, t_fs.at[way], t_far.at[g, a, q], y_to[way])
                tap_share(g, a, q, dy)

    def tap_far(a, q):
        for g in range(2):
            arrived(slab(g, a, wrap(y + 2), q, 2 * c, 2), t_far.at[g, a, q])
            tap_share(g, a, q, 2)

    def tap_partner(q):
        for g in range(2):
            rows = pl.ds(pl.multiple_of((4 * q + 2 * (1 - c)) * QT, QT), 2 * QT)
            arrived(taps.at[g, rows], t_pp.at[g, q])

    def tap_left():
        left(taps.at[0], t_ps)
        for way in range(2):
            left(taps.at[0, pl.ds(0, 512)], t_ys.at[way])
            left(taps.at[0, pl.ds(0, 256)], t_fs.at[way])

    def w_block(g, p, half=None):
        if half is None:
            return wts.at[g, pl.ds(pl.multiple_of(p * XB, XB), XB)]
        n = XB // 2
        return wts.at[g, pl.ds(pl.multiple_of(p * XB + half * n, n), n)]

    def w_out():
        for e in range(3):
            for g in range(2):
                q = 3 * z + e
                if g == 0:
                    to, i = lax.rem(q, 4), lax.div(q, 4)
                else:
                    to, i = lax.rem(q + x, 4), e
                rows = pl.ds(pl.multiple_of((3 * cross[g] + i) * UNIT, UNIT), UNIT)
                send_or_copy(
                    weight.at[pl.ds((2 * e + g) * UNIT, UNIT)], wts.at[g, rows],
                    w_as.at[g, e], w_own.at[g], on_ring(g, to, c), to == ring[g],
                )

    def w_sides():
        for g in range(2):
            here = w_block(g, cross[g])
            arrived(here, w_own.at[g])
            for way in range(2):
                send(here, here, w_ss.at[g, way], w_side.at[g, way], cross_to[g][way])

    def w_forward():
        for g in range(2):
            for way in range(2):
                p = wrap(cross[g] + (3, 1)[way])
                arrived(w_block(g, p), w_side.at[g, way])
                half = w_block(g, p, way)
                send(half, half, w_fs.at[g, way], w_d2.at[g], cross_to[g][way])

    def w_far():
        for g in range(2):
            arrived(w_block(g, wrap(cross[g] + 2)), w_d2.at[g])

    def w_left():
        for g in range(2):
            for way in range(2):
                left(w_block(g, 0), w_ss.at[g, way])
                left(w_block(g, 0, 0), w_fs.at[g, way])

    def down_dot(i):
        code_copy(i).wait()
        part = dot(act_v[...], codes_v[i % SLOTS])
        n = i // 2
        if i % 2 == 0:
            d_ps[n] = part.astype(BF)
        else:
            d_own[n] = part
        if i + SLOTS < 8:
            code_copy(i + SLOTS).start()

    def down_share(n):
        send(d_ps.at[n], d_pr.at[n], dp_send.at[n], dp_recv.at[n], partner)

    def down_block(i):
        down_dot(i)
        if i % 2 == 0:
            down_share(i // 2)

    def down_far(h):
        for way in range(2):
            rows = slice(h * HT + way * FT, h * HT + way * FT + FT)
            d_hs[h, way] = (d_own[0, rows] + d_pr[0, rows].astype(F32)).astype(BF)
            send(d_hs.at[h, way], d_hr.at[h, way], dh_send.at[h, way], dh_recv.at[h, way], y_to[way])

    def down_sides(h):
        for way in range(2):
            n = 1 + way
            arrived(d_hr.at[h, way], dh_recv.at[h, way])
            for half in range(2):
                rows = slice(h * HT + half * FT, h * HT + half * FT + FT)
                value = d_own[n, rows] + d_pr[n, rows].astype(F32)
                if half == way:
                    value = value + d_hr[h, way].astype(F32)
                d_bs[h, way, half * FT : half * FT + FT] = value.astype(BF)
            send(d_bs.at[h, way], d_br.at[h, way], db_send.at[h, way], db_recv.at[h, way], y_to[way])

    def down_end(h):
        for way in range(2):
            arrived(d_br.at[h, way], db_recv.at[h, way])
        rows = slice(h * HT, h * HT + HT)
        row_full = jnp.broadcast_to(act_scale[:, rows], (128, HT)).T[:, :1]
        col_full = col_v[...].astype(F32) * QUANT_UNIT
        down = d_own[3, rows] + d_pr[3, rows].astype(F32)
        down = down + d_br[h, 0].astype(F32) + d_br[h, 1].astype(F32)
        high_v[rows] = (res_v[rows].astype(F32) + down * row_full * col_full).astype(BF)
        for q in range(h * NQ // 2, (h + 1) * NQ // 2):
            tap_out(2, q, high_v)

    def down_left():
        for n in range(4):
            left(d_ps.at[n], dp_send.at[n])
        for h in range(2):
            for way in range(2):
                left(d_hs.at[h, way], dh_send.at[h, way])
                left(d_bs.at[h, way], db_send.at[h, way])

    def join_start(q):
        tap_partner(q)
        for g in range(2):
            rows = pl.ds(4 * q * QT, 4 * QT)
            j_s[q, g] = dot(taps[g, rows], wts[g]).astype(BF)
            for r in (2, 1, 3):
                to = wrap(ring[g] + r)
                send(
                    j_s.at[q, g, pl.ds(pl.multiple_of(to * QT, QT), QT)], j_r.at[q, g, r - 1],
                    j_send, j_recv.at[q], on_ring(g, to, c),
                )

    def join_end(q):
        arrived(j_r.at[q], j_recv.at[q])
        rows = slice(q * QT, q * QT + QT)
        joined = jnp.zeros((QT, COL), F32)
        for g in range(2):
            joined = joined + j_s[q, g, pl.ds(pl.multiple_of(ring[g] * QT, QT), QT)].astype(F32)
            for r in range(3):
                joined = joined + j_r[q, g, r].astype(F32)
        j_v[rows] = joined
        grad_norm = go_v[rows].astype(F32) * gain[...]
        lane = lax.broadcasted_iota(jnp.int32, (QT, 128), 1)
        squares = jnp.sum(joined * joined, axis=1, keepdims=True)
        inner = jnp.sum(grad_norm * joined, axis=1, keepdims=True)
        both = jnp.where(lane == 0, squares, jnp.where(lane == 1, inner, 0.0))
        st_s[q] = both.T[:8]
        for r in range(1, 8):
            send(
                st_s.at[q], st_r.at[q, r - 1], st_send, st_recv.at[q],
                {"tensor": lax.rem(t + r, 8), "seq": s},
            )

    def g_piece(g, q, n, r):
        cols = pl.ds(pl.multiple_of((4 * q + r) * QT, QT), QT)
        return gt_v.at[g, pl.ds(n * CW, CW), cols]

    def norm(q):
        arrived(st_r.at[q], st_recv.at[q])
        rows = slice(q * QT, q * QT + QT)
        total = st_s[q]
        for r in range(7):
            total = total + st_r[q, r]
        both = jnp.concatenate([total, jnp.zeros((120, QT), F32)], axis=0).T
        inverse_rms = lax.rsqrt(both[:, 0:1] / D + 1e-05)
        projection = inverse_rms * both[:, 1:2] / D
        normed = j_v[rows] * inverse_rms
        grad_norm = go_v[rows].astype(F32) * gain[...]
        grad_joined = inverse_rms * (grad_norm - normed * projection)
        turned = grad_joined.T.astype(BF)
        for g in range(2):
            gt_v[g, :, pl.ds(pl.multiple_of((4 * q + ring[g]) * QT, QT), QT)] = turned
        for n in range(CHUNKS):
            for g in range(2):
                here = g_piece(g, q, n, ring[g])
                for r in (2, 1, 3):
                    send(
                        here, here, a_send, a_recv.at[g, q, n, r - 1],
                        on_ring(g, wrap(ring[g] + r), c),
                    )
        drafted_v[rows] = (normed * gain[...]).astype(BF)

    def grad_part(g, n, p):
        cols = pl.ds(pl.multiple_of(wrap(cross[g] + p) * XB, XB), XB)
        return dot(gt_v[g, n * CW : n * CW + CW], taps[g, :, cols])

    def grad_start(n):
        for g in range(2):
            for q in range(NQ):
                for r in range(1, 4):
                    arrived(g_piece(g, q, n, wrap(ring[g] - r)), a_recv.at[g, q, n, r - 1])
            part = grad_part(g, n, 2).astype(BF)
            for way in range(2):
                g_hs[n, g, way] = part[way * CH : way * CH + CH]
                send(
                    g_hs.at[n, g, way], g_hr.at[n, g, way], gh_send,
                    gh_recv.at[n, g, way], cross_to[g][way],
                )

    def grad_sides(n):
        for g in range(2):
            for way in range(2):
                part = grad_part(g, n, (1, 3)[way])
                arrived(g_hr.at[n, g, way], gh_recv.at[n, g, way])
                for half in range(2):
                    rows = slice(half * CH, half * CH + CH)
                    value = part[rows]
                    if half == way:
                        value = value + g_hr[n, g, way].astype(F32)
                    g_bs[n, g, way, rows] = value.astype(BF)
                send(
                    g_bs.at[n, g, way], g_br.at[n, g, way], gb_send,
                    gb_recv.at[n, g], cross_to[g][way],
                )

    def grad_own(n):
        for g in range(2):
            g_own[n, g] = grad_part(g, n, 0)

    def grad_end(n):
        for g in range(2):
            arrived(g_br.at[n, g], gb_recv.at[n, g])
            total = g_own[n, g] + g_br[n, g, 0].astype(F32) + g_br[n, g, 1].astype(F32)
            f_s[n, g] = total.T.astype(BF)
            for i in range(3):
                if g == 0:
                    q = 4 * i + z
                    to, e = lax.div(q, 3), lax.rem(q, 3)
                else:
                    to, e = wrap(x + z - i), i
                rows = pl.ds(pl.multiple_of((2 * e + g) * UNIT, UNIT), UNIT)
                send_or_copy(
                    f_s.at[n, g, pl.ds(i * UNIT, UNIT)],
                    grad_join.at[rows, pl.ds(n * CW, CW)],
                    f_send.at[n, g, i], f_recv.at[n], on_ring(g, to, c), to == ring[g],
                )

    act_copy.wait()
    down_dot(0)
    pl.semaphore_wait(barrier, greeted)
    tap_out(0, 0, tap_low)
    tap_out(1, 0, tap_mid)
    down_share(0)
    w_out()
    for q in range(1, NQ):
        tap_out(0, q, tap_low)
        tap_out(1, q, tap_mid)
    down_block(1)
    down_block(2)
    tap_own(0, 0)
    arrived(d_pr.at[0], dp_recv.at[0])
    down_far(0)
    down_far(1)
    down_block(3)
    tap_own(1, 0)
    w_sides()
    down_block(4)
    down_block(5)
    tap_own(0, 1)
    for n in (1, 2):
        arrived(d_pr.at[n], dp_recv.at[n])
    down_sides(0)
    down_sides(1)
    tap_sides(0, 0)
    down_block(6)
    tap_sides(1, 0)
    down_block(7)
    tap_own(1, 1)
    w_forward()
    tap_far(0, 0)
    tap_far(1, 0)
    arrived(d_pr.at[3], dp_recv.at[3])
    res_copy.wait()
    col_copy.wait()
    down_end(0)
    tap_sides(0, 1)
    down_end(1)
    tap_own(2, 0)
    tap_sides(1, 1)
    tap_own(2, 1)
    go_copy.wait()
    w_far()
    tap_sides(2, 0)
    tap_own(0, 2)
    tap_far(0, 1)
    tap_far(1, 1)
    tap_sides(2, 1)
    tap_own(1, 2)
    tap_far(2, 0)
    join_start(0)
    tap_own(2, 2)
    tap_far(2, 1)
    join_start(1)
    tap_sides(0, 2)
    tap_own(0, 3)
    tap_sides(1, 2)
    join_end(0)
    tap_own(1, 3)
    tap_sides(2, 2)
    tap_own(2, 3)
    norm(0)
    tap_far(0, 2)
    tap_far(1, 2)
    join_end(1)
    tap_sides(0, 3)
    tap_far(2, 2)
    join_start(2)
    norm(1)
    tap_sides(1, 3)
    tap_sides(2, 3)
    join_end(2)
    tap_far(0, 3)
    tap_far(1, 3)
    norm(2)
    tap_far(2, 3)
    join_start(3)
    drain()
    down_left()
    w_left()
    join_end(3)
    tap_left()
    norm(3)
    drafted_copy = pltpu.make_async_copy(drafted_v, drafted, l_sem.at[4])
    drafted_copy.start()
    for n in range(CHUNKS):
        grad_start(n)
    for n in range(CHUNKS):
        grad_sides(n)
        grad_own(n)
    left(j_r, j_send)
    left(st_r, st_send)
    left(taps.at[0, pl.ds(0, 1024)], a_send)
    for n in range(CHUNKS):
        grad_end(n)

    left(g_hs, gh_send)
    left(g_bs, gb_send)
    drain()
    drafted_copy.wait()
    for n in range(CHUNKS):
        arrived(grad_join.at[:, pl.ds(n * CW, CW)], f_recv.at[n])


def on_device(
    tap_low, tap_mid, residual_in, ffn_act, act_scale, down_codes, down_scale,
    join_weight, join_gain, grad_out,
):
    any_ = pl.BlockSpec(memory_space=pl.ANY)
    vmem = pl.BlockSpec(memory_space=pltpu.VMEM)
    V = pltpu.VMEM
    dma = lambda *shape: pltpu.SemaphoreType.DMA(shape)
    one = pltpu.SemaphoreType.DMA
    scratch = [
        V((TOK, HID), BF), V((SLOTS, HID, COL), BF), V((1, COL), jnp.int32),
        V((TOK, COL), BF), V((TOK, COL), BF),
        V((2, 4 * TOK, KG), BF), V((2, KG, COL), BF),
        V((4, TOK, COL), F32), V((4, TOK, COL), BF), V((4, TOK, COL), BF),
        V((2, 2, FT, COL), BF), V((2, 2, FT, COL), BF),
        V((2, 2, HT, COL), BF), V((2, 2, HT, COL), BF),
        V((TOK, COL), BF),
        V((NQ, 2, 4 * QT, COL), BF), V((NQ, 2, 3, QT, COL), BF),
        V((TOK, COL), F32), V((NQ, 8, QT), F32), V((NQ, 7, 8, QT), F32), V((TOK, COL), BF),
        V((2, COL, 4 * TOK), BF), V((CHUNKS, 2, CW, XB), F32),
        V((CHUNKS, 2, 2, CH, XB), BF), V((CHUNKS, 2, 2, CH, XB), BF),
        V((CHUNKS, 2, 2, CW, XB), BF), V((CHUNKS, 2, 2, CW, XB), BF),
        V((CHUNKS, 2, XB, CW), BF),
        dma(5), dma(SLOTS),
        dma(2, 3, NQ), dma(2, 3, NQ, 2), dma(2, 3, NQ), dma(2, NQ),
        dma(2, 3, NQ, 2), dma(2), dma(2), one,
        dma(2), dma(2, 3), dma(2, 2), dma(2), dma(2, 2), dma(2, 2),
        dma(4), dma(4), dma(2, 2), dma(2, 2), dma(2, 2), dma(2, 2),
        dma(NQ), one, dma(NQ), one, dma(2, NQ, CHUNKS, 3), one,
        dma(CHUNKS, 2, 2), one, dma(CHUNKS, 2), one,
        dma(CHUNKS), dma(CHUNKS, 2, 3),
    ]
    return pl.pallas_call(
        body,
        out_shape=(
            jax.ShapeDtypeStruct((TOK, COL), BF),
            jax.ShapeDtypeStruct((2 * XB, COL), BF),
        ),
        in_specs=[any_, any_, any_, any_, vmem, any_, any_, any_, vmem, any_],
        out_specs=(any_, any_),
        scratch_shapes=scratch,
        compiler_params=pltpu.CompilerParams(
            collective_id=0, has_side_effects=True, vmem_limit_bytes=63 * 1024 * 1024
        ),
        cost_estimate=pl.CostEstimate(
            flops=20_400_000_000, bytes_accessed=30_000_000, transcendentals=0
        ),
        name="tapped_join",
    )(
        tap_low, tap_mid, residual_in, ffn_act, act_scale.reshape(1, TOK), down_codes,
        down_scale.reshape(1, D), join_weight, join_gain.reshape(1, COL), grad_out,
    )


def solution(mesh):
    return jax.shard_map(
        on_device,
        mesh=mesh,
        in_specs=(
            P("seq", "tensor"),
            P("seq", "tensor"),
            P("seq", "tensor"),
            P("seq", "tensor"),
            P("seq"),
            P("tensor", None),
            P(),
            P("seq", "tensor"),
            P("tensor"),
            P("seq", "tensor"),
        ),
        out_specs=(P("seq", "tensor"), P("seq", "tensor")),
        check_vma=False,
    )
```

time: 170 us -> 147 us (0.86)
  Pallas kernels: 165 us -> 142 us
    pallas_call x1, Pallas kernels: 165 us -> 142 us  [on_device(): pl.pallas_call(body, out_shape=(jax.ShapeDtypeStruct((TOK, COL), BF), jax...]
where the time goes in v3:
time: 147 us; the launch traced here: 146 us
  Pallas kernels  142 us (97%)
  local copies, waits for them, and re-layouts  3.93 us (3%)
    pallas_call x1, Pallas kernels, on_device(): pl.pallas_call(body, out_shape=(jax.ShapeDtypeStruct((TOK, COL), BF), jax...  142 us
    unnamed x2, local copies, waits for them, and re-layouts  3.93 us

profile of v3, /device:TPU:0, one launch (start us, length us, event | category | flops | bytes accessed | tf_op | source)
XLA Modules:
  0.0 146.5 jit_solution(16287053821792927000)
XLA Ops:
  0.6 141.9 %tapped_join.1 = (bf16[512,512]{1,0:T(8,128)(2,1)}, bf16[768,512]{1,0:T(8,128)(2,1)}) custom-call(bf16[512,512]{1,0:T(8,128)(2,1)} %tap_low.1, bf16[512,512]{1,0:T(8,128)(2,1)} %tap_mid.1, bf16[512,512]{1,0:T(8,128)(2,1)} %residual.1, bf16[512,1792]{1,0:T(8,128)(2,1)} %act.1, f32[1,512]{1,0:T(1,128)} %bitcast.4, bf16[1792,4096]{1,0:T(8,128)(2,1)} %codes.1, ...), custom_call_target="tpu_custom_call" | custom-call | flops 20400001024 | bytes 30000000 | tf_op jit(solution)/shard_map/tapped_join/pallas_call | solution.py:571
  142.6 1.9 %copy.14 = bf16[512,512]{1,0:T(8,128)(2,1)} copy(bf16[512,512]{1,0:T(8,128)(2,1)} %get-tuple-element.4) | data formatting | bytes 1048576
  144.4 2.1 %copy.15 = bf16[768,512]{1,0:T(8,128)(2,1)} copy(bf16[768,512]{1,0:T(8,128)(2,1)} %get-tuple-element.5) | data formatting | bytes 1572864

commit v4 on v3

--- a/solution.py
+++ b/solution.py
@@ -440,6 +440,7 @@
     for q in range(1, NQ):
         tap_out(0, q, tap_low)
         tap_out(1, q, tap_mid)
+
     down_block(1)
     down_block(2)
     tap_own(0, 0)
@@ -451,11 +452,11 @@
     w_sides()
     down_block(4)
     down_block(5)
-    tap_own(0, 1)
     for n in (1, 2):
         arrived(d_pr.at[n], dp_recv.at[n])
     down_sides(0)
     down_sides(1)
+    tap_own(0, 1)
     tap_sides(0, 0)
     down_block(6)
     tap_sides(1, 0)
@@ -472,49 +473,50 @@
     down_end(1)
     tap_own(2, 0)
     tap_sides(1, 1)
+    w_far()
+    go_copy.wait()
+    tap_sides(2, 0)
     tap_own(2, 1)
-    go_copy.wait()
-    w_far()
-    tap_sides(2, 0)
-    tap_own(0, 2)
     tap_far(0, 1)
     tap_far(1, 1)
+    tap_own(0, 2)
+    tap_far(2, 0)
+    join_start(0)
     tap_sides(2, 1)
     tap_own(1, 2)
-    tap_far(2, 0)
-    join_start(0)
     tap_own(2, 2)
     tap_far(2, 1)
     join_start(1)
     tap_sides(0, 2)
+    join_end(0)
+    tap_sides(1, 2)
     tap_own(0, 3)
-    tap_sides(1, 2)
-    join_end(0)
+    tap_sides(2, 2)
+    norm(0)
     tap_own(1, 3)
-    tap_sides(2, 2)
+    tap_far(0, 2)
     tap_own(2, 3)
-    norm(0)
-    tap_far(0, 2)
+    join_end(1)
     tap_far(1, 2)
-    join_end(1)
-    tap_sides(0, 3)
     tap_far(2, 2)
     join_start(2)
+    tap_sides(0, 3)
     norm(1)
     tap_sides(1, 3)
     tap_sides(2, 3)
+    tap_far(0, 3)
     join_end(2)
-    tap_far(0, 3)
     tap_far(1, 3)
-    norm(2)
     tap_far(2, 3)
     join_start(3)
+    norm(2)
     drain()
     down_left()
     w_left()
     join_end(3)
     tap_left()
     norm(3)
+
     drafted_copy = pltpu.make_async_copy(drafted_v, drafted, l_sem.at[4])
     drafted_copy.start()
     for n in range(CHUNKS):
@@ -534,6 +536,11 @@
     drafted_copy.wait()
     for n in range(CHUNKS):
         arrived(grad_join.at[:, pl.ds(n * CW, CW)], f_recv.at[n])
+
+
+def hand_on(drafted, grad_join, drafted_out, grad_join_out):
+    drafted_out[...] = drafted[...]
+    grad_join_out[...] = grad_join[...]
 
 
 def on_device(
@@ -568,12 +575,13 @@
         dma(CHUNKS, 2, 2), one, dma(CHUNKS, 2), one,
         dma(CHUNKS), dma(CHUNKS, 2, 3),
     ]
-    return pl.pallas_call(
+    shapes = (
+        jax.ShapeDtypeStruct((TOK, COL), BF),
+        jax.ShapeDtypeStruct((2 * XB, COL), BF),
+    )
+    results = pl.pallas_call(
         body,
-        out_shape=(
-            jax.ShapeDtypeStruct((TOK, COL), BF),
-            jax.ShapeDtypeStruct((2 * XB, COL), BF),
-        ),
+        out_shape=shapes,
         in_specs=[any_, any_, any_, any_, vmem, any_, any_, any_, vmem, any_],
         out_specs=(any_, any_),
         scratch_shapes=scratch,
@@ -588,6 +596,13 @@
         tap_low, tap_mid, residual_in, ffn_act, act_scale.reshape(1, TOK), down_codes,
         down_scale.reshape(1, D), join_weight, join_gain.reshape(1, COL), grad_out,
     )
+    return pl.pallas_call(
+        hand_on,
+        out_shape=shapes,
+        in_specs=[vmem, vmem],
+        out_specs=(vmem, vmem),
+        name="hand_on",
+    )(*results)
 
 
 def solution(mesh):

time: 147 us -> 139 us (0.946)
  Pallas kernels: 142 us -> 138 us
  local copies, waits for them, and re-layouts: 3.93 us -> 0 us
    pallas_call x1 -> x2, Pallas kernels: 142 us -> 138 us  [the longest x1 136 us: on_device(): pl.pallas_call(body, out_shape=shapes, in_specs=[any_, any_, any_, any_,...]
    unnamed x2 -> x0, local copies, waits for them, and re-layouts: 3.93 us -> none
where the time goes in v4:
time: 139 us
  Pallas kernels  138 us (99%)
    pallas_call x1, Pallas kernels, on_device(): pl.pallas_call(body, out_shape=shapes, in_specs=[any_, any_, any_, any_,...  136 us

profile of v4, /device:TPU:0, one launch (start us, length us, event | category | flops | bytes accessed | tf_op | source)
XLA Modules:
  0.0 138.6 jit_solution(15931248265191877506)
XLA Ops:
  0.6 135.6 %tapped_join.1 = (bf16[512,512]{1,0:T(8,128)(2,1)}, bf16[768,512]{1,0:T(8,128)(2,1)}) custom-call(bf16[512,512]{1,0:T(8,128)(2,1)} %tap_low.1, bf16[512,512]{1,0:T(8,128)(2,1)} %tap_mid.1, bf16[512,512]{1,0:T(8,128)(2,1)} %residual.1, bf16[512,1792]{1,0:T(8,128)(2,1)} %act.1, f32[1,512]{1,0:T(1,128)} %bitcast.4, bf16[1792,4096]{1,0:T(8,128)(2,1)} %codes.1, ...), custom_call_target="tpu_custom_call" | custom-call | flops 20400001024 | bytes 30000000 | tf_op jit(solution)/shard_map/tapped_join/pallas_call | solution.py:582
  136.2 2.4 %hand_on.1 = (bf16[512,512]{1,0:T(8,128)(2,1)}, bf16[768,512]{1,0:T(8,128)(2,1)}) custom-call(bf16[512,512]{1,0:T(8,128)(2,1)} %get-tuple-element.4.drafted, bf16[768,512]{1,0:T(8,128)(2,1)} %get-tuple-element.5.grad_join), custom_call_target="tpu_custom_call" | custom-call | tf_op jit(solution)/shard_map/hand_on/pallas_call | solution.py:599

commit v5 on v4

--- a/solution.py
+++ b/solution.py
@@ -113,6 +113,21 @@
         cols = pl.ds(pl.multiple_of(code_block(i) * COL, COL), COL)
         return pltpu.make_async_copy(codes.at[:, cols], codes_v.at[i % SLOTS], c_sem.at[i % SLOTS])
 
+    barrier = pltpu.get_barrier_semaphore()
+    greeted = 0
+
+    def greet(device):
+        pl.semaphore_signal(barrier, inc=1, device_id=device, device_id_type=MESH)
+
+    for r in range(1, 8):
+        greet({"tensor": lax.rem(t + r, 8), "seq": s})
+        greeted += 1
+    for g in range(2):
+        for r in range(1, 4):
+            for cc in range(2):
+                greet(on_ring(g, wrap(ring[g] + r), cc))
+                greeted += 1
+
     act_copy = pltpu.make_async_copy(act, act_v, l_sem.at[0])
     act_copy.start()
     for i in range(SLOTS):
@@ -125,21 +140,6 @@
         col_code.at[:, pl.ds(pl.multiple_of(t * COL, COL), COL)], col_v, l_sem.at[3]
     )
     col_copy.start()
-
-    barrier = pltpu.get_barrier_semaphore()
-    greeted = 0
-
-    def greet(device):
-        pl.semaphore_signal(barrier, inc=1, device_id=device, device_id_type=MESH)
-
-    for r in range(1, 8):
-        greet({"tensor": lax.rem(t + r, 8), "seq": s})
-        greeted += 1
-    for g in range(2):
-        for r in range(1, 4):
-            for cc in range(2):
-                greet(on_ring(g, wrap(ring[g] + r), cc))
-                greeted += 1
 
     def place(g, a, ys):
         n = 4 * a + ys
@@ -375,15 +375,37 @@
                     )
         drafted_v[rows] = (normed * gain[...]).astype(BF)
 
+    def grad_cols(g, p):
+        return pl.ds(pl.multiple_of(wrap(cross[g] + p) * XB, XB), XB)
+
+    def grad_early(first, last):
+        span = slice(4 * first * QT, 4 * last * QT)
+        for n in range(CHUNKS):
+            for g in range(2):
+                for q in range(first, last):
+                    g_wait(g, q, n)
+
+                def add(p, _):
+                    part = dot(gt_v[g, n * CW : n * CW + CW, span], taps[g, span, grad_cols(g, p)])
+                    if first > 0:
+                        part = part + g_own[n, g, p]
+                    g_own[n, g, p] = part
+                    return 0
+
+                lax.fori_loop(0, 4, add, 0)
+
+    def g_wait(g, q, n):
+        for r in range(1, 4):
+            arrived(g_piece(g, q, n, wrap(ring[g] - r)), a_recv.at[g, q, n, r - 1])
+
     def grad_part(g, n, p):
-        cols = pl.ds(pl.multiple_of(wrap(cross[g] + p) * XB, XB), XB)
-        return dot(gt_v[g, n * CW : n * CW + CW], taps[g, :, cols])
+        span = slice(4 * (NQ - 1) * QT, 4 * NQ * QT)
+        part = dot(gt_v[g, n * CW : n * CW + CW, span], taps[g, span, grad_cols(g, p)])
+        return part + g_own[n, g, p]
 
     def grad_start(n):
         for g in range(2):
-            for q in range(NQ):
-                for r in range(1, 4):
-                    arrived(g_piece(g, q, n, wrap(ring[g] - r)), a_recv.at[g, q, n, r - 1])
+            g_wait(g, NQ - 1, n)
             part = grad_part(g, n, 2).astype(BF)
             for way in range(2):
                 g_hs[n, g, way] = part[way * CH : way * CH + CH]
@@ -410,12 +432,12 @@
 
     def grad_own(n):
         for g in range(2):
-            g_own[n, g] = grad_part(g, n, 0)
+            g_own[n, g, 0] = grad_part(g, n, 0)
 
     def grad_end(n):
         for g in range(2):
             arrived(g_br.at[n, g], gb_recv.at[n, g])
-            total = g_own[n, g] + g_br[n, g, 0].astype(F32) + g_br[n, g, 1].astype(F32)
+            total = g_own[n, g, 0] + g_br[n, g, 0].astype(F32) + g_br[n, g, 1].astype(F32)
             f_s[n, g] = total.T.astype(BF)
             for i in range(3):
                 if g == 0:
@@ -430,11 +452,11 @@
                     f_send.at[n, g, i], f_recv.at[n], on_ring(g, to, c), to == ring[g],
                 )
 
-    act_copy.wait()
-    down_dot(0)
     pl.semaphore_wait(barrier, greeted)
     tap_out(0, 0, tap_low)
     tap_out(1, 0, tap_mid)
+    act_copy.wait()
+    down_dot(0)
     down_share(0)
     w_out()
     for q in range(1, NQ):
@@ -442,8 +464,8 @@
         tap_out(1, q, tap_mid)
 
     down_block(1)
+    tap_own(0, 0)
     down_block(2)
-    tap_own(0, 0)
     arrived(d_pr.at[0], dp_recv.at[0])
     down_far(0)
     down_far(1)
@@ -513,9 +535,11 @@
     drain()
     down_left()
     w_left()
+    grad_early(0, 2)
     join_end(3)
     tap_left()
     norm(3)
+    grad_early(2, 3)
 
     drafted_copy = pltpu.make_async_copy(drafted_v, drafted, l_sem.at[4])
     drafted_copy.start()
@@ -523,13 +547,13 @@
         grad_start(n)
     for n in range(CHUNKS):
         grad_sides(n)
+    for n in range(CHUNKS):
         grad_own(n)
+        grad_end(n)
+
     left(j_r, j_send)
     left(st_r, st_send)
     left(taps.at[0, pl.ds(0, 1024)], a_send)
-    for n in range(CHUNKS):
-        grad_end(n)
-
     left(g_hs, gh_send)
     left(g_bs, gb_send)
     drain()
@@ -562,7 +586,7 @@
         V((TOK, COL), BF),
         V((NQ, 2, 4 * QT, COL), BF), V((NQ, 2, 3, QT, COL), BF),
         V((TOK, COL), F32), V((NQ, 8, QT), F32), V((NQ, 7, 8, QT), F32), V((TOK, COL), BF),
-        V((2, COL, 4 * TOK), BF), V((CHUNKS, 2, CW, XB), F32),
+        V((2, COL, 4 * TOK), BF), V((CHUNKS, 2, 4, CW, XB), F32),
         V((CHUNKS, 2, 2, CH, XB), BF), V((CHUNKS, 2, 2, CH, XB), BF),
         V((CHUNKS, 2, 2, CW, XB), BF), V((CHUNKS, 2, 2, CW, XB), BF),
         V((CHUNKS, 2, XB, CW), BF),

time: 139 us -> 135 us (0.971)
  Pallas kernels: 138 us -> 134 us
    pallas_call x1, Pallas kernels: 136 us -> 131 us  [on_device(): pl.pallas_call(body, out_shape=shapes, in_specs=[any_, any_, any_, any_,...]
where the time goes in v5:
time: 135 us; the launch traced here: 134 us
  Pallas kernels  134 us (99%)
    pallas_call x1, Pallas kernels, on_device(): pl.pallas_call(body, out_shape=shapes, in_specs=[any_, any_, any_, any_,...  131 us

profile of v5, /device:TPU:0, one launch (start us, length us, event | category | flops | bytes accessed | tf_op | source)
XLA Modules:
  0.0 134.4 jit_solution(8552867157245273380)
XLA Ops:
  0.6 131.4 %tapped_join.1 = (bf16[512,512]{1,0:T(8,128)(2,1)}, bf16[768,512]{1,0:T(8,128)(2,1)}) custom-call(bf16[512,512]{1,0:T(8,128)(2,1)} %tap_low.1, bf16[512,512]{1,0:T(8,128)(2,1)} %tap_mid.1, bf16[512,512]{1,0:T(8,128)(2,1)} %residual.1, bf16[512,1792]{1,0:T(8,128)(2,1)} %act.1, f32[1,512]{1,0:T(1,128)} %bitcast.4, bf16[1792,4096]{1,0:T(8,128)(2,1)} %codes.1, ...), custom_call_target="tpu_custom_call" | custom-call | flops 20400001024 | bytes 30000000 | tf_op jit(solution)/shard_map/tapped_join/pallas_call | solution.py:606
  132.0 2.4 %hand_on.1 = (bf16[512,512]{1,0:T(8,128)(2,1)}, bf16[768,512]{1,0:T(8,128)(2,1)}) custom-call(bf16[512,512]{1,0:T(8,128)(2,1)} %get-tuple-element.4.drafted, bf16[768,512]{1,0:T(8,128)(2,1)} %get-tuple-element.5.grad_join), custom_call_target="tpu_custom_call" | custom-call | tf_op jit(solution)/shard_map/hand_on/pallas_call | solution.py:623
